TPU v7x, 512 devices: a whole 4x4x16 slice. The times are simulated.
512 devices in a mesh: blk: 128 (over x, z, core), gz: 4 (over y).
Axes of the slice: x: 4, y: 4, z: 16, core: 2. Of those that a mesh axis runs over, the one named last changes fastest.
Arguments:
- fixed: bfloat16 [128, 32, 32, 128], P('blk', 'gz'), may hold values from -6 to 6
- moving: bfloat16 [128, 32, 32, 128], P('blk', 'gz'), may hold values from -6 to 6
- block_place: int32 [128], P('blk'), may hold values from 0 to 127, each once
- tissue: int32 [128], P('blk'), may hold values 0 or 1
Outputs:
- velocity: float32 [3, 2, 32, 64], replicated
- cc_map: float32 [128, 32, 32, 128], P('blk', 'gz')
Inputs may be any that keep to these rules, and one draw needn't show every extreme that they name: `block_place`: each block position from 0 to 127 is named by exactly one block.
All inputs are finite; a program needn't handle non-finite values. No bound on the sum of `tissue` on one device may be relied on, other than what follows from the above.
Results may differ from a plain program's by a relative error of at most 0.0004.
Values may be sent and summed in bfloat16 or wider, within the bound.
A program may use at most 64 MiB of HBM per device.

v0:
```python
import math

import jax
import jax.numpy as jnp
from jax import lax
from jax.sharding import PartitionSpec as P

SCALE = 16
GY = 8
ITERS = 2


EXACT = lax.Precision.HIGHEST
EPSILON = 1e-05
STEP_LENGTH = 0.5
BOX_TAPS = [1.0 / 9.0] * 9
GAUSS_RAW = [math.exp(-((offset - 3) ** 2) / 4.5) for offset in range(7)]
GAUSS_TAPS = [value / sum(GAUSS_RAW) for value in GAUSS_RAW]


def with_halo(block, sides, width):
    for axis, dim in sides:
        count = lax.axis_size(axis)
        forward = [(i, i + 1) for i in range(count - 1)]
        backward = [(target, source) for source, target in forward]
        low = lax.ppermute(
            lax.slice_in_dim(block, block.shape[dim] - width, None, axis=dim), axis, forward
        )
        high = lax.ppermute(lax.slice_in_dim(block, 0, width, axis=dim), axis, backward)
        block = jnp.concatenate([low, block, high], axis=dim)
    return block


def tap_matrix(count, taps):
    radius = len(taps) // 2
    rows = jnp.arange(count)[:, None]
    cols = jnp.arange(count)[None, :]
    matrix = jnp.zeros((count, count), jnp.float32)
    for offset, weight in enumerate(taps):
        matrix = matrix + weight * (rows - cols == offset - radius).astype(jnp.float32)
    return matrix


def along_rows(field, matrix):
    return jnp.einsum("...xy,xu->...uy", field, matrix, precision=EXACT)


def along_cols(field, matrix):
    return jnp.einsum("...y,yv->...v", field, matrix, precision=EXACT)


def planes_filter(field, taps, count):
    total = jnp.zeros(field.shape[:-3] + (count,) + field.shape[-2:], jnp.float32)
    for offset, weight in enumerate(taps):
        total = total + weight * field[..., offset : offset + count, :, :]
    return total


def slope(field, axis):
    widths = [(0, 0)] * field.ndim
    widths[axis] = (1, 1)
    padded = jnp.pad(field, widths)
    length = field.shape[axis]
    upper = lax.slice_in_dim(padded, 2, length + 2, axis=axis)
    lower = lax.slice_in_dim(padded, 0, length, axis=axis)
    return 0.5 * (upper - lower)


def hat_rows(coords, count):
    where = jnp.clip((coords + 0.5) / SCALE - 0.5, 0.0, count - 1.0)
    marks = jnp.arange(count).astype(jnp.float32)
    return jnp.maximum(0.0, 1.0 - jnp.abs(where[..., None] - marks))


def statistics(means, fixed_c, warped_c):
    sii = means[2] - means[0] * means[0]
    sww = means[3] - means[1] * means[1]
    siw = means[4] - means[0] * means[1]
    denom = sii * sww + EPSILON
    similar = siw * siw / denom
    weight = (
        2.0 * siw / denom * (fixed_c - means[0] - siw / (sww + EPSILON) * (warped_c - means[1]))
    )
    return (similar, weight)


def smooth_axis(field, axis):
    widths = [(0, 0)] * field.ndim
    widths[axis] = (1, 1)
    padded = jnp.pad(field, widths)
    length = field.shape[axis]
    upper = lax.slice_in_dim(padded, 2, length + 2, axis=axis)
    lower = lax.slice_in_dim(padded, 0, length, axis=axis)
    return 0.25 * lower + 0.5 * field + 0.25 * upper


def regularize(velocity, total, coarse_rows, coarse_cols):
    block_rows = velocity.shape[2] // coarse_rows
    coarse_depth = velocity.shape[1]
    grid = total.reshape(block_rows, GY, 3, coarse_depth, coarse_rows, coarse_cols)
    grid = grid.transpose(2, 3, 0, 4, 1, 5).reshape(velocity.shape)
    regular = smooth_axis(smooth_axis(smooth_axis(grid, 1), 2), 3)
    return velocity + STEP_LENGTH * regular / jnp.sqrt(jnp.mean(regular * regular) + EPSILON)


def per_device(fixed, moving, block_place, tissue):
    slots, planes, row_side, col_side = fixed.shape
    depth_parts = lax.axis_size("gz")
    depth_index = lax.axis_index("gz")
    blocks = slots * lax.axis_size("blk")
    total_planes = planes * depth_parts
    coarse_depth = total_planes // SCALE
    coarse_rows = row_side // SCALE
    coarse_cols = col_side // SCALE
    grid_rows = blocks // GY * coarse_rows
    grid_cols = GY * coarse_cols
    stacked = jnp.stack([fixed, moving], 0)
    reach = 0
    haloed = with_halo(stacked, (("gz", 2),), 5)
    images = haloed.astype(jnp.float32)
    count_w = planes + 2 * (reach + 4)
    count_m = planes + 2 * reach
    fixed_w = images[0, :, 1 : 1 + count_w]
    moving_w = images[1, :, 1 : 1 + count_w]
    depth_slope = 0.5 * (images[1, :, 2 : 2 + count_w] - images[1, :, 0:count_w])
    row_slope = slope(moving_w, 2)
    col_slope = slope(moving_w, 3)
    depth_w = depth_index * planes - (reach + 4) + jnp.arange(count_w)
    inside_w = ((depth_w >= 0) & (depth_w < total_planes)).astype(jnp.float32)
    depth_hat = hat_rows(depth_w.astype(jnp.float32), coarse_depth)
    depth_m = depth_index * planes - reach + jnp.arange(count_m)
    inside_m = ((depth_m >= 0) & (depth_m < total_planes)).astype(jnp.float32)
    row_cells = jnp.arange(row_side)
    col_cells = jnp.arange(col_side)
    block_row = block_place // GY
    block_col = block_place % GY
    row_hat = hat_rows(
        (block_row[:, None] * row_side + row_cells[None, :]).astype(jnp.float32), grid_rows
    )
    col_hat = hat_rows(
        (block_col[:, None] * col_side + col_cells[None, :]).astype(jnp.float32), grid_cols
    )
    own_depth = depth_index * planes + jnp.arange(planes)
    restrict = (own_depth[None, :] // SCALE == jnp.arange(coarse_depth)[:, None]).astype(
        jnp.float32
    )
    box_rows = tap_matrix(row_side, BOX_TAPS)
    box_cols = tap_matrix(col_side, BOX_TAPS)
    gauss_rows = tap_matrix(row_side, GAUSS_TAPS)
    gauss_cols = tap_matrix(col_side, GAUSS_TAPS)
    tissue_scale = tissue.astype(jnp.float32)[:, None, None, None]
    positions = jnp.arange(blocks)
    velocity = jnp.zeros((3, coarse_depth, grid_rows, grid_cols), jnp.float32)
    correlation = jnp.zeros((slots, planes, row_side, col_side), jnp.float32)
    for rounds in range(ITERS):
        partial_value = jnp.einsum("ckab,sxa->sckxb", velocity, row_hat, precision=EXACT)
        partial_value = jnp.einsum("sckxb,syb->sckxy", partial_value, col_hat, precision=EXACT)
        shift = jnp.einsum("zk,sckxy->cszxy", depth_hat, partial_value, precision=EXACT)
        warped = moving_w + shift[0] * depth_slope + shift[1] * row_slope + shift[2] * col_slope
        warped = warped * inside_w[None, :, None, None]
        fields = jnp.stack(
            [fixed_w, warped, fixed_w * fixed_w, warped * warped, fixed_w * warped], 0
        )
        means = planes_filter(fields, BOX_TAPS, count_m)
        means = along_cols(along_rows(means, box_rows), box_cols)
        fixed_m = fixed_w[:, 4 : 4 + count_m]
        warped_m = warped[:, 4 : 4 + count_m]
        similar, weight = statistics(means, fixed_m, warped_m)
        scale = weight * tissue_scale * inside_m[None, :, None, None]
        depth_grad = 0.5 * (warped[:, 5 : 5 + count_m] - warped[:, 3 : 3 + count_m])
        force = jnp.stack(
            [scale * depth_grad, scale * slope(warped_m, 2), scale * slope(warped_m, 3)], 0
        )
        force = with_halo(force, (("gz", 2),), 3)
        smooth = planes_filter(force, GAUSS_TAPS, planes)
        smooth = along_cols(along_rows(smooth, gauss_rows), gauss_cols)
        local = smooth.reshape(3, slots, planes, coarse_rows, SCALE, coarse_cols, SCALE).sum(
            axis=(4, 6)
        )
        piece = jnp.einsum("kp,cspab->sckab", restrict, local, precision=EXACT).reshape(slots, -1)
        onehot_local = (positions[:, None] == block_place[None, :]).astype(jnp.float32)
        local_grid = jnp.dot(onehot_local, piece, precision=EXACT)
        total = lax.psum(local_grid, ("blk", "gz"))
        velocity = regularize(velocity, total, coarse_rows, coarse_cols)
        correlation = similar
    return (velocity, correlation)


def solution(mesh):
    return jax.shard_map(
        per_device,
        mesh=mesh,
        in_specs=(P("blk", "gz", None, None), P("blk", "gz", None, None), P("blk"), P("blk")),
        out_specs=(P(), P("blk", "gz", None, None)),
        check_vma=False,
    )
```

profile of v0, /device:TPU:1, one launch (start us, length us, event | category | flops | bytes accessed | tf_op | source)
XLA Modules:
  0.0 267.4 jit_solution(6952006898740505339)
XLA Ops:
  0.6 0.9 copy_bitcast_fusion
  1.6 4.0 %collective-permute-start = (bf16[2,1,5,32,128]{4,2,3,1,0:T(8,128)(2,1)S(1)}, bf16[2,1,5,32,128]{4,2,3,1,0:T(8,128)(2,1)S(1)}, u32[]{:S(2)}, u32[]{:S(2)}) collective-permute-start(bf16[2,1,5,32,128]{4,2,3,1,0:T(8,128)(2,1)S(1)} %get-tuple-element.38), channel_id=1, source_target_pairs={{0,1},{1,2},{2,3},{4,5},{5,6},{6,7},{8,9},{9,10},{10,11},{12,13},{... | collective-permute-start | bytes 245768 | tf_op jit(solution)/shard_map/ppermute | solution.py:26
  5.7 1.3 collective-permute-start.1
  8.6 0.3 convolution_bitcast_fusion.4
  9.0 0.3 fusion.117
  9.3 0.9 fusion.94
  10.2 1.2 collective-permute-done.1
  11.4 0.2 maximum_convert_fusion
  11.7 0.2 bitcast_dynamic-update-slice_fusion.5
  12.1 0.5 fusion.3
  12.6 0.7 convolution_bitcast_fusion.2
  13.3 1.0 fusion.6
  14.3 0.2 fusion.70
  14.7 3.5 %collective-permute-start.2 = (f32[3,1,3,32,128]{4,2,3,1,0:T(4,128)S(1)}, f32[3,1,3,32,128]{4,2,3,1,0:T(4,128)S(1)}, u32[]{:S(2)}, u32[]{:S(2)}) collective-permute-start(f32[3,1,3,32,128]{4,2,3,1,0:T(4,128)S(1)} %get-tuple-element.30), channel_id=1, source_target_pairs={{0,1},{1,2},{2,3},{4,5},{5,6},{6,7},{8,9},{9,10},{10,11},{12,13},{... | collective-permute-start | bytes 442376 | tf_op jit(solution)/shard_map/ppermute | solution.py:26
  18.2 1.3 collective-permute-start.3
  19.6 1.3 collective-permute-done.2
  20.8 3.8 %collective-permute-done.3 = f32[3,1,3,32,128]{4,2,3,1,0:T(4,128)S(1)} collective-permute-done((f32[3,1,3,32,128]{4,2,3,1,0:T(4,128)S(1)}, f32[3,1,3,32,128]{4,2,3,1,0:T(4,128)S(1)}, u32[]{:S(2)}, u32[]{:S(2)}) %collective-permute-start.3) | collective-permute-done | bytes 147488 | tf_op jit(solution)/shard_map/ppermute | solution.py:29
  24.8 0.3 fusion.18
  25.1 0.5 fusion.26
  25.6 3.3 %convolution_reduce_fusion.1 = f32[3,8,2,8]{3,2,1,0:T(2,128)S(1)} fusion(f32[3,8,2,16,128,1]{4,3,5,2,1,0:T(8,128)S(1)} %bitcast.237, f32[8,16,128,1,1,1]{2,1,0,5,4,3:T(8,128)S(1)} %bitcast.238), kind=kOutput, calls=%fused_computation.1 | convolution fusion | flops 151092864 | bytes 460288 | tf_op jit(solution)/shard_map/...y,yv->...v/dot_general | solution.py:49
  29.3 0.4 reshape.689
  29.7 1.2 copy.70
  31.0 1.4 reshape.690
  32.3 111.2 %psum.14 = f32[3,2,32,64]{3,2,1,0:T(8,128)S(1)} all-reduce(f32[3,2,32,64]{3,2,1,0:T(8,128)S(1)} %reshape.690), channel_id=1, replica_groups=mesh['blk'=128,'gz'=4] {'blk','gz'}, use_global_device_ids=true, to_apply=%region_1.2 | all-reduce | flops 12288 | bytes 98304 | tf_op jit(solution)/shard_map/psum | solution.py:183
  143.6 0.7 multiply_reduce_fusion.1
  145.1 0.4 convolution_bitcast_fusion.3
  145.4 0.3 fusion.115
  145.8 0.9 convolution_bitcast_fusion
  146.7 0.2 bitcast_dynamic-update-slice_fusion.2
  147.0 0.5 fusion.1
  147.5 0.7 convolution_bitcast_fusion.1
  148.2 1.0 fusion.4
  149.3 0.1 fusion.65
  149.7 1.4 collective-permute-start.4
  151.1 1.3 collective-permute-start.5
  152.4 0.7 copy.84
  153.1 1.5 collective-permute-done.4
  154.6 3.8 %collective-permute-done.5 = f32[3,1,3,32,128]{4,2,3,1,0:T(4,128)S(1)} collective-permute-done((f32[3,1,3,32,128]{4,2,3,1,0:T(4,128)S(1)}, f32[3,1,3,32,128]{4,2,3,1,0:T(4,128)S(1)}, u32[]{:S(2)}, u32[]{:S(2)}) %collective-permute-start.5) | collective-permute-done | bytes 147488 | tf_op jit(solution)/shard_map/ppermute | solution.py:29
  158.4 0.2 maximum_maximum_fusion.1
  158.5 0.3 fusion.11
  158.9 0.5 fusion.24
  159.3 3.3 %convolution_reduce_fusion = f32[3,8,2,8]{3,2,1,0:T(2,128)S(1)} fusion(f32[3,8,2,16,128,1]{4,3,5,2,1,0:T(8,128)S(1)} %bitcast.236, f32[8,16,128,1,1,1]{2,1,0,5,4,3:T(8,128)S(1)} %bitcast.239), kind=kOutput, calls=%fused_computation | convolution fusion | flops 151092864 | bytes 460288 | tf_op jit(solution)/shard_map/...y,yv->...v/dot_general | solution.py:49
  163.0 0.4 reshape.697
  163.4 0.3 copy.83
  163.8 0.2 reshape.698
  164.0 101.1 %psum.15 = f32[3,2,32,64]{3,2,1,0:T(8,128)S(1)} all-reduce(f32[3,2,32,64]{3,2,1,0:T(8,128)S(1)} %reshape.698), channel_id=1, replica_groups=mesh['blk'=128,'gz'=4] {'blk','gz'}, use_global_device_ids=true, to_apply=%region_4.5 | all-reduce | flops 12288 | bytes 98304 | tf_op jit(solution)/shard_map/psum | solution.py:183
  265.2 0.7 multiply_reduce_fusion
  266.6 0.8 divide_add_fusion
  (51 shorter events, 2.1 us)
Async XLA Ops:
  1.6 8.6 %collective-permute-start = (bf16[2,1,5,32,128]{4,2,3,1,0:T(8,128)(2,1)S(1)}, bf16[2,1,5,32,128]{4,2,3,1,0:T(8,128)(2,1)S(1)}, u32[]{:S(2)}, u32[]{:S(2)}) collective-permute-start(bf16[2,1,5,32,128]{4,2,3,1,0:T(8,128)(2,1)S(1)} %get-tuple-element.38), channel_id=1, source_target_pairs={{0,1},{1,2},{2,3},{4,5},{5,6},{6,7},{8,9},{9,10},{10,11},{12,13},{... | collective-permute-start | bytes 245768 | tf_op jit(solution)/shard_map/ppermute | solution.py:26
  5.7 5.7 %collective-permute-start.1 = (bf16[2,1,5,32,128]{4,2,3,1,0:T(8,128)(2,1)S(1)}, bf16[2,1,5,32,128]{4,2,3,1,0:T(8,128)(2,1)S(1)}, u32[]{:S(2)}, u32[]{:S(2)}) collective-permute-start(bf16[2,1,5,32,128]{4,2,3,1,0:T(8,128)(2,1)S(1)} %get-tuple-element.39), channel_id=1, source_target_pairs={{1,0},{2,1},{3,2},{5,4},{6,5},{7,6},{9,8},{10,9},{11,10},{13,12},{... | collective-permute-start | bytes 245768 | tf_op jit(solution)/shard_map/ppermute | solution.py:29
  7.6 2.6 copy-start
  7.8 2.4 copy-start.2
  14.7 6.1 %collective-permute-start.2 = (f32[3,1,3,32,128]{4,2,3,1,0:T(4,128)S(1)}, f32[3,1,3,32,128]{4,2,3,1,0:T(4,128)S(1)}, u32[]{:S(2)}, u32[]{:S(2)}) collective-permute-start(f32[3,1,3,32,128]{4,2,3,1,0:T(4,128)S(1)} %get-tuple-element.30), channel_id=1, source_target_pairs={{0,1},{1,2},{2,3},{4,5},{5,6},{6,7},{8,9},{9,10},{10,11},{12,13},{... | collective-permute-start | bytes 442376 | tf_op jit(solution)/shard_map/ppermute | solution.py:26
  18.2 6.4 %collective-permute-start.3 = (f32[3,1,3,32,128]{4,2,3,1,0:T(4,128)S(1)}, f32[3,1,3,32,128]{4,2,3,1,0:T(4,128)S(1)}, u32[]{:S(2)}, u32[]{:S(2)}) collective-permute-start(f32[3,1,3,32,128]{4,2,3,1,0:T(4,128)S(1)} %get-tuple-element.31), channel_id=1, source_target_pairs={{1,0},{2,1},{3,2},{5,4},{6,5},{7,6},{9,8},{10,9},{11,10},{13,12},{... | collective-permute-start | bytes 442376 | tf_op jit(solution)/shard_map/ppermute | solution.py:29
  29.7 115.3 %copy-start.1 = (f32[32]{0:T(128)S(1)}, f32[32]{0:T(128)}, u32[]{:S(2)}) copy-start(f32[32]{0:T(128)} %copy-done) | copy-start | bytes 388
  29.7 115.3 %copy-start.3 = (f32[32]{0:T(128)S(1)}, f32[32]{0:T(128)}, u32[]{:S(2)}) copy-start(f32[32]{0:T(128)} %copy-done.2) | copy-start | bytes 388
  149.7 4.9 %collective-permute-start.4 = (f32[3,1,3,32,128]{4,2,3,1,0:T(4,128)S(1)}, f32[3,1,3,32,128]{4,2,3,1,0:T(4,128)S(1)}, u32[]{:S(2)}, u32[]{:S(2)}) collective-permute-start(f32[3,1,3,32,128]{4,2,3,1,0:T(4,128)S(1)} %get-tuple-element.26), channel_id=1, source_target_pairs={{0,1},{1,2},{2,3},{4,5},{5,6},{6,7},{8,9},{9,10},{10,11},{12,13},{... | collective-permute-start | bytes 442376 | tf_op jit(solution)/shard_map/ppermute | solution.py:26
  151.1 7.3 %collective-permute-start.5 = (f32[3,1,3,32,128]{4,2,3,1,0:T(4,128)S(1)}, f32[3,1,3,32,128]{4,2,3,1,0:T(4,128)S(1)}, u32[]{:S(2)}, u32[]{:S(2)}) collective-permute-start(f32[3,1,3,32,128]{4,2,3,1,0:T(4,128)S(1)} %get-tuple-element.27), channel_id=1, source_target_pairs={{1,0},{2,1},{3,2},{5,4},{6,5},{7,6},{9,8},{10,9},{11,10},{13,12},{... | collective-permute-start | bytes 442376 | tf_op jit(solution)/shard_map/ppermute | solution.py:29
where the time goes:
time: 268 us; the launch traced here: 267 us
  blocking collectives  212 us (79%)
  matrix products  14.4 us (5%)
  starting transfers between devices  12.8 us (5%)
  waiting for transfers between devices  11.6 us (4%)
  local copies, waits for them, and re-layouts  6.26 us (2%)
  other arithmetic  6.11 us (2%)
  between operations  3.95 us (1%)
    psum x2, blocking collectives, per_device(): total = lax.psum(local_grid, ('blk', 'gz'))  212 us
    ppermute x3, starting transfers between devices, with_halo(): lax.ppermute(lax.slice_in_dim(block, block.shape[dim] - width, None, axis...  8.92 us
    ppermute x3, waiting for transfers between devices, with_halo(): lax.ppermute(lax.slice_in_dim(block, 0, width, axis=dim), axis, backward)  8.79 us
    dot_general x4, matrix products, along_cols(): return jnp.einsum('...y,yv->...v', field, matrix, precision=EXACT)  8.73 us
  transfers between devices with their start and end apart: 6, of which 5 were waited for; matrix products, arithmetic and copies ran while one was open for 1% of the time, Pallas kernels for 0%

commit v1 on v0

v1 whole, which is shorter than its diff:
```python
import functools
import math

import jax
import jax.numpy as jnp
from jax import lax
from jax.experimental import pallas as pl
from jax.experimental.pallas import tpu as pltpu
from jax.sharding import PartitionSpec as P

NX, NY, NZC = 4, 4, 16
F32, BF16 = jnp.float32, jnp.bfloat16
EPSILON = 1e-05
STEP_LENGTH = 0.5
RAW = [math.exp(-(t * t) / 4.5) for t in range(4)]
TOTAL = RAW[0] + 2 * (RAW[1] + RAW[2] + RAW[3])
W1, W2, W3 = (RAW[t] / TOTAL for t in (1, 2, 3))
PLACE_LANE = 48
MESH = pl.DeviceIdType.MESH


def coordinates():
    blk = lax.axis_index("blk")
    return blk // (2 * NZC), lax.axis_index("gz"), (blk // 2) % NZC, blk % 2


def device(x, y, z, core):
    return ((x * NZC + z) * 2 + core, y)


def peers():
    x, y, z, core = coordinates()
    along_y = [device(x, (y + d) % NY, z, core) for d in range(1, NY)]
    along_z = [device(x, y, (z + d) % NZC, core) for d in range(1, NZC)]
    along_x = [device((x + d // 2) % NX, y, z, (core + d) % 2) for d in range(1, 2 * NX)]
    return along_y, along_z, along_x


def iota(shape, dim):
    return lax.broadcasted_iota(jnp.int32, shape, dim)


def split(value):
    high = value.astype(BF16)
    return high, (value - high.astype(F32)).astype(BF16)


def group_weight(t):
    near = jnp.minimum(t, 15 - t)
    out = jnp.where(near >= 3, 1.0, 0.0)
    for at, value in (
        (2, 1 - W3),
        (1, 1 - W3 - W2),
        (0, 1 - W3 - W2 - W1),
        (-1, W1 + W2 + W3),
        (-2, W2 + W3),
        (-3, W3),
    ):
        out = jnp.where(near == at, value, out)
    return out


def hat_tri(where, mark):
    gap = where - mark
    hat = lambda d: jnp.maximum(0.0, 1.0 - jnp.abs(d))
    return 0.5 * hat(gap) + 0.25 * (hat(gap - 1.0) + hat(gap + 1.0))


def window_sums(planes):
    two = [planes[i] + planes[i + 1] for i in range(15)]
    four = [two[i] + two[i + 2] for i in range(13)]
    eight = [four[i] + four[i + 4] for i in range(8)]
    return [eight[i] + planes[i + 8] for i in range(8)]


def shifted(value, amount, dim):
    size = value.shape[dim]
    at = iota(value.shape, dim)
    edge = 0 if amount == 1 else size - 1
    return jnp.where(at == edge, 0.0, pltpu.roll(value, amount % size, dim))


def kernel(
    fixed_hbm, moving_hbm, place_ref, tissue_ref,
    velocity_ref, cc_hbm,
    own_i, own_j, halo_i, halo_j,
    image_i, image_j, slope_x, slope_y, warped_ref,
    box_rows, box_cols, grad_rows, grad_cols, gauss_cols, spread,
    sums, means, stat_i, cc_ref, expanded,
    rows_y, rows_z, local_sem, halo_send, halo_recv, gather_send, gather_recv,
):
    x, y, z, core = coordinates()
    gz = y
    along_y, along_z, along_x = peers()
    barrier = pltpu.get_barrier_semaphore()
    for peer in along_y + along_z + along_x:
        pl.semaphore_signal(barrier, inc=1, device_id=peer, device_id_type=MESH)
    load_i = pltpu.make_async_copy(fixed_hbm.at[0], own_i, local_sem.at[0])
    load_j = pltpu.make_async_copy(moving_hbm.at[0], own_j, local_sem.at[1])
    load_i.start()
    load_j.start()

    r, c = iota((256, 256), 0), iota((256, 256), 1)
    same = (r >> 5) == (c >> 5)
    box_rows[...] = jnp.where(same & (jnp.abs(r - c) <= 4), 1.0, 0.0).astype(BF16)
    grad_rows[...] = jnp.where(
        same & (c - r == 1), 0.5, jnp.where(same & (r - c == 1), -0.5, 0.0)
    ).astype(BF16)
    r, c = iota((128, 128), 0), iota((128, 128), 1)
    band = jnp.where(jnp.abs(r - c) <= 4, 1.0, 0.0).astype(BF16)
    box_cols[0:128, :] = band
    box_cols[128:256, :] = band
    grad_cols[...] = jnp.where(r - c == 1, 0.5, jnp.where(c - r == 1, -0.5, 0.0)).astype(BF16)
    high, low = split(group_weight(r - 16 * (c & 7)))
    gauss_cols[0:128, :] = high
    gauss_cols[128:256, :] = high
    gauss_cols[256:384, :] = low
    r, c = iota((128, 768), 0), iota((128, 768), 1)
    half = jnp.where(c >= 384, 1, 0)
    c = c - 384 * half
    pick = ((r >> 6) == half) & (((r >> 3) & 7) == (c >> 6)) & ((r & 7) == (c & 7))
    pick = jnp.where(pick, 1.0, 0.0).astype(BF16)
    spread[0:128, :] = pick
    spread[128:256, :] = pick

    load_i.wait()
    load_j.wait()
    pl.semaphore_wait(barrier, len(along_y) + len(along_z) + len(along_x))

    up, down = along_y[0], along_y[2]
    halos = []
    for index, (source, target, peer) in enumerate(
        (
            (own_j.at[3:8], halo_j.at[0], up),
            (own_j.at[0:5], halo_j.at[1], down),
            (own_i.at[4:8], halo_i.at[0], up),
            (own_i.at[0:4], halo_i.at[1], down),
        )
    ):
        copy = pltpu.make_async_remote_copy(
            source, target, halo_send.at[index], halo_recv.at[index],
            device_id=peer, device_id_type=MESH,
        )
        copy.start()
        halos.append(copy)

    inside_low = jnp.where(gz > 0, 1.0, 0.0)
    inside_high = jnp.where(gz < NY - 1, 1.0, 0.0)
    for p in range(8):
        image_i[4 + p] = own_i[p].astype(F32)
        image_j[5 + p] = own_j[p].astype(F32)
    flat = own_j[...].reshape(256, 128)
    slope_x[128:384, :] = jnp.dot(grad_rows[...], flat, preferred_element_type=F32)
    slope_y[128:384, :] = jnp.dot(flat, grad_cols[...], preferred_element_type=F32)

    for copy in halos:
        copy.wait_recv()
    for p in range(5):
        image_j[p] = halo_j[0, p].astype(F32) * inside_low
        image_j[13 + p] = halo_j[1, p].astype(F32) * inside_high
    for p in range(4):
        image_i[p] = halo_i[0, p].astype(F32) * inside_low
        image_i[12 + p] = halo_i[1, p].astype(F32) * inside_high

    def box_sums(slot):
        field = jnp.dot(box_rows[...], sums[slot], preferred_element_type=F32)
        high, low = split(field[:, :128] + field[:, 128:])
        field = jnp.dot(high, box_cols[0:128, :], preferred_element_type=F32) + jnp.dot(
            low, box_cols[0:128, :], preferred_element_type=F32
        )
        return field * (1.0 / 729.0)

    def put_sums(slot, chunk, planes):
        for p, value in enumerate(window_sums(planes)):
            high, low = split(value)
            at = pl.ds(32 * p + 16 * chunk, 16)
            sums[slot, at, 0:128] = high
            sums[slot, at, 128:256] = low

    depth_weight = []
    for p in range(8):
        at = gz * 8 + p
        first = group_weight(at)
        second = group_weight(at - 16)
        depth_weight.append((0.5 * first + 0.25 * second, 0.25 * first + 0.5 * second))
    lane = iota((32, 128), 1)
    lane_group = (lane >> 3) & 7
    row_weight = group_weight(iota((32, 128), 0) - 16 * (lane >> 6))
    place = place_ref[0]
    tissue = tissue_ref[0].astype(F32)

    def piece(planes, first):
        totals = [None] * 6
        for p in range(8):
            at = pl.ds(32 * p, 32)
            mean_i, var_i = stat_i[0, at, :], stat_i[1, at, :]
            mean_w = means[0, at, :]
            var_w = means[1, at, :] - mean_w * mean_w
            cov = means[2, at, :] - mean_i * mean_w
            denom = var_i * var_w + EPSILON
            ratio = cov / denom
            if not first:
                cc_ref[p] = cov * ratio
            image = image_i[4 + p]
            mid = planes[4 + p]
            dcc = 2.0 * ratio * (image - mean_i - cov / (var_w + EPSILON) * (mid - mean_w))
            if first:
                along_rows = slope_x[128 + 32 * p : 160 + 32 * p, :]
                along_cols = slope_y[128 + 32 * p : 160 + 32 * p, :]
            else:
                along_rows = 0.5 * (shifted(mid, -1, 0) - shifted(mid, 1, 0))
                along_cols = 0.5 * (shifted(mid, -1, 1) - shifted(mid, 1, 1))
            along_depth = 0.5 * (planes[5 + p] - planes[3 + p])
            for c, slope in enumerate((along_depth, along_rows, along_cols)):
                force = dcc * slope
                for k in range(2):
                    term = depth_weight[p][k] * force
                    totals[2 * c + k] = term if p == 0 else totals[2 * c + k] + term
        merged = jnp.zeros((32, 128), F32)
        for ck in range(6):
            high, low = split(totals[ck])
            part = (
                jnp.dot(high, gauss_cols[0:128, :], preferred_element_type=F32)
                + jnp.dot(low, gauss_cols[0:128, :], preferred_element_type=F32)
                + jnp.dot(high, gauss_cols[256:384, :], preferred_element_type=F32)
            )
            merged = jnp.where(lane_group == ck, part, merged)
        row = jnp.sum(merged * row_weight, axis=0, keepdims=True) * tissue
        lane_row = iota((1, 128), 1)
        return jnp.where(lane_row == PLACE_LANE, place.astype(F32) * 0.25, row)

    unsent = []

    def exchange(source, targets, everything, sem, partners):
        for d, peer in enumerate(partners):
            pltpu.make_async_remote_copy(
                source, targets(d + 1), gather_send.at[sem], gather_recv.at[sem],
                device_id=peer, device_id_type=MESH,
            ).start()
        done = pltpu.make_async_remote_copy(
            everything, everything, gather_send.at[sem], gather_recv.at[sem],
            device_id=partners[0], device_id_type=MESH,
        )
        done.wait_recv()
        unsent.append(done)

    def gather(turn, row):
        one, many = rows_y.at[turn], rows_z.at[turn]
        rows_y[turn, 0] = row
        exchange(one.at[0], lambda d: one.at[d], one.at[1:NY], 3 * turn, along_y)
        rows_z[turn, 0, 0] = (rows_y[turn, 0] + rows_y[turn, 2]) + (
            rows_y[turn, 1] + rows_y[turn, 3]
        )
        exchange(
            many.at[0, 0], lambda d: many.at[0, d], many.at[0, 1:NZC], 3 * turn + 1, along_z
        )
        exchange(many.at[0], lambda d: many.at[d], many.at[1 : 2 * NX], 3 * turn + 2, along_x)
        return rows_z[turn].reshape(128, 128)

    for chunk in range(2):
        at = pl.ds(16 * chunk, 16)
        fixed = [image_i[p, at, :] for p in range(16)]
        put_sums(0, chunk, fixed)
        put_sums(1, chunk, [value * value for value in fixed])
        moved = [image_j[1 + p, at, :] for p in range(16)]
        put_sums(2, chunk, moved)
        put_sums(3, chunk, [value * value for value in moved])
        put_sums(4, chunk, [a * b for a, b in zip(fixed, moved)])
    mean_i = box_sums(0)
    stat_i[0] = mean_i
    stat_i[1] = box_sums(1) - mean_i * mean_i
    for slot in range(3):
        means[slot] = box_sums(2 + slot)
    row = piece([image_j[1 + p] for p in range(16)], True)
    gathered = gather(0, row)

    for start, side, offset in ((0, 0, 1), (384, 1, 0)):
        flat = halo_j[side, offset : offset + 4].reshape(128, 128)
        slope_x[start : start + 128, :] = jnp.dot(
            grad_rows[0:128, 0:128], flat, preferred_element_type=F32
        )
        slope_y[start : start + 128, :] = jnp.dot(
            flat, grad_cols[...], preferred_element_type=F32
        )

    spot = jnp.broadcast_to(gathered[:, PLACE_LANE : PLACE_LANE + 1], (128, 128)).astype(jnp.int32)
    r, c = iota((128, 128), 0), iota((128, 128), 1)
    in_column = (spot & 7) == ((c >> 3) & 7)
    spot_row = jnp.sum(jnp.where(r == c, spot, 0).astype(F32), axis=0, keepdims=True).astype(
        jnp.int32
    )
    mark = ((spot_row >> 3) * 2).astype(F32)
    mark = jnp.broadcast_to(jnp.concatenate([mark, mark + 1.0], axis=1), (64, 256))
    at = iota((64, 256), 0)
    own_row, own_col = place >> 3, place & 7
    inner = (own_row * 32 + at - 32).astype(F32)
    inner = jnp.clip((inner + 0.5) * (1.0 / 16.0) - 0.5, 0.0, 31.0)
    where = jnp.where(at < 32, at.astype(F32), inner)
    combine = hat_tri(where, mark).astype(BF16)
    r, c = iota((128, 256), 0), iota((128, 256), 1)
    inner = (own_col * 128 + (c & 127)).astype(F32)
    inner = jnp.clip((inner + 0.5) * (1.0 / 16.0) - 0.5, 0.0, 63.0)
    to_cols = jnp.where(
        (r >> 6) == (c >> 7), hat_tri(inner, (r & 63).astype(F32)), 0.0
    ).astype(BF16)

    def grid_of(gathered, count):
        high, low = split(gathered)
        wide = jnp.dot(high, spread[0:128, :], preferred_element_type=F32) + jnp.dot(
            low, spread[0:128, :], preferred_element_type=F32
        )
        for tile in range(6):
            value = jnp.where(in_column, wide[:, 128 * tile : 128 * tile + 128], 0.0)
            high, low = split(value)
            at = 128 * (tile // 3)
            lanes = pl.ds(128 * (tile % 3), 128)
            expanded[at : at + 128, lanes] = high
            expanded[256 + at : 384 + at, lanes] = low
        left = combine[0:count]
        return jnp.dot(left, expanded[0:256, :], preferred_element_type=F32) + jnp.dot(
            left, expanded[256:512, :], preferred_element_type=F32
        )

    def regular_of(grid):
        out = []
        at = iota((32, 128), 1) & 63
        squares = jnp.zeros((32, 128), F32)
        for tile in range(3):
            value = grid[:, 128 * tile : 128 * tile + 128]
            left = jnp.where(at == 0, 0.0, pltpu.roll(value, 1, 1))
            right = jnp.where(at == 63, 0.0, pltpu.roll(value, 127, 1))
            value = 0.5 * value + 0.25 * (left + right)
            squares = squares + value * value
            out.append(value)
        mean = jnp.sum(squares, keepdims=True) * (1.0 / (6 * 32 * 64))
        return out, STEP_LENGTH / jnp.sqrt(mean + EPSILON)

    grid = grid_of(gathered, 64)
    regular, scale = regular_of(grid[0:32])
    before = [value * scale for value in regular]
    shift = []
    for tile in range(3):
        high, low = split(grid[32:64, 128 * tile : 128 * tile + 128])
        value = jnp.dot(high, to_cols, preferred_element_type=F32) + jnp.dot(
            low, to_cols, preferred_element_type=F32
        )
        value = value * scale
        shift.append((value[:, :128], value[:, 128:] - value[:, :128]))

    for p in range(16):
        deep = (gz * 8 + (p - 4)).astype(F32)
        part = jnp.clip((deep + 0.5) * (1.0 / 16.0) - 0.5, 0.0, 1.0)
        value = image_j[1 + p]
        slopes = (
            0.5 * (image_j[2 + p] - image_j[p]),
            slope_x[32 * p : 32 * p + 32, :],
            slope_y[32 * p : 32 * p + 32, :],
        )
        for (base, rise), slope in zip(shift, slopes):
            value = value + (base + part * rise) * slope
        if p < 4:
            value = value * inside_low
        if p >= 12:
            value = value * inside_high
        warped_ref[p] = value
    for chunk in range(2):
        at = pl.ds(16 * chunk, 16)
        moved = [warped_ref[p, at, :] for p in range(16)]
        put_sums(2, chunk, moved)
        put_sums(3, chunk, [value * value for value in moved])
        put_sums(4, chunk, [image_i[p, at, :] * value for p, value in enumerate(moved)])
    for slot in range(3):
        means[slot] = box_sums(2 + slot)
    row = piece([warped_ref[p] for p in range(16)], False)
    store = pltpu.make_async_copy(cc_ref, cc_hbm.at[0], local_sem.at[0])
    store.start()
    gathered = gather(1, row)
    regular, scale = regular_of(grid_of(gathered, 32))
    for tile in range(3):
        value = before[tile] + regular[tile] * scale
        velocity_ref[tile, 0] = value[:, 0:64]
        velocity_ref[tile, 1] = value[:, 64:128]
    for copy in halos:
        copy.wait_send()
    for copy in unsent:
        copy.wait_send()
    store.wait()


def per_device(fixed, moving, block_place, tissue):
    vmem = pltpu.VMEM
    return pl.pallas_call(
        kernel,
        out_shape=(
            jax.ShapeDtypeStruct((3, 2, 32, 64), F32),
            jax.ShapeDtypeStruct((1, 8, 32, 128), F32),
        ),
        in_specs=[
            pl.BlockSpec(memory_space=pl.ANY),
            pl.BlockSpec(memory_space=pl.ANY),
            pl.BlockSpec(memory_space=pltpu.SMEM),
            pl.BlockSpec(memory_space=pltpu.SMEM),
        ],
        out_specs=(
            pl.BlockSpec(memory_space=pltpu.VMEM),
            pl.BlockSpec(memory_space=pl.ANY),
        ),
        scratch_shapes=[
            vmem((8, 32, 128), BF16),
            vmem((8, 32, 128), BF16),
            vmem((2, 4, 32, 128), BF16),
            vmem((2, 5, 32, 128), BF16),
            vmem((16, 32, 128), F32),
            vmem((18, 32, 128), F32),
            vmem((512, 128), F32),
            vmem((512, 128), F32),
            vmem((16, 32, 128), F32),
            vmem((256, 256), BF16),
            vmem((256, 128), BF16),
            vmem((256, 256), BF16),
            vmem((128, 128), BF16),
            vmem((384, 128), BF16),
            vmem((256, 768), BF16),
            vmem((5, 256, 256), BF16),
            vmem((3, 256, 128), F32),
            vmem((2, 256, 128), F32),
            vmem((8, 32, 128), F32),
            vmem((512, 384), BF16),
            vmem((2, NY, 1, 128), F32),
            vmem((2, 2 * NX, NZC, 1, 128), F32),
            pltpu.SemaphoreType.DMA((2,)),
            pltpu.SemaphoreType.DMA((4,)),
            pltpu.SemaphoreType.DMA((4,)),
            pltpu.SemaphoreType.DMA((6,)),
            pltpu.SemaphoreType.DMA((6,)),
        ],
        compiler_params=pltpu.CompilerParams(
            collective_id=0, has_side_effects=True, vmem_limit_bytes=32 * 1024 * 1024
        ),
    )(fixed, moving, block_place, tissue)


def solution(mesh):
    return jax.shard_map(
        per_device,
        mesh=mesh,
        in_specs=(P("blk", "gz", None, None), P("blk", "gz", None, None), P("blk"), P("blk")),
        out_specs=(P(), P("blk", "gz", None, None)),
        check_vma=False,
    )
```

time: 268 us -> 60.5 us (0.23)
  blocking collectives: 212 us -> 0 us
  Pallas kernels: 0 us -> 55.3 us
  matrix products: 14.4 us -> 0 us
  starting transfers between devices: 12.8 us -> 0 us
  waiting for transfers between devices: 11.6 us -> 0 us
  other arithmetic: 6.11 us -> 0 us
  local copies, waits for them, and re-layouts: 6.26 us -> 2.97 us
    psum x2 -> x0, blocking collectives: 212 us -> none  [per_device(): total = lax.psum(local_grid, ('blk', 'gz'))]
    pallas_call x0 -> x1, Pallas kernels: none -> 55.3 us  [per_device(): pl.pallas_call(kernel, out_shape=(jax.ShapeDtypeStruct((3, 2, 32, 64), F3...]
    dot_general x16 -> x0, matrix products: 14.4 us -> none  [the longest x4 8.73 us: along_cols(): return jnp.einsum('...y,yv->...v', field, matrix, precision=EXACT)]
    ppermute x6 -> x0, starting transfers between devices: 12.8 us -> none  [the longest x3 8.92 us: with_halo(): lax.ppermute(lax.slice_in_dim(block, block.shape[dim] - width, None, axis...]
    ppermute x6 -> x0, waiting for transfers between devices: 11.6 us -> none  [the longest x3 8.79 us: with_halo(): lax.ppermute(lax.slice_in_dim(block, 0, width, axis=dim), axis, backward)]
  transfers between devices with their start and end apart: 6 -> 0, of which waited for: 5 -> 0; matrix products, arithmetic and copies ran while one was open for 1% -> 0% of each run, Pallas kernels for 0% -> 0%
where the time goes in v1:
time: 60.5 us; the launch traced here: 60.2 us
  Pallas kernels  55.3 us (91%)
  local copies, waits for them, and re-layouts  2.97 us (5%)
  between operations  1.94 us (3%)
    pallas_call x1, Pallas kernels, per_device(): pl.pallas_call(kernel, out_shape=(jax.ShapeDtypeStruct((3, 2, 32, 64), F3...  55.3 us
    unnamed x6, local copies, waits for them, and re-layouts  2.97 us

profile of v1, /device:TPU:1, one launch (start us, length us, event | category | flops | bytes accessed | tf_op | source)
XLA Modules:
  0.0 60.2 jit_solution(8185854866316033173)
XLA Ops:
  1.9 0.0 copy-start
  1.9 0.8 %copy-done = bf16[1,8,32,128]{3,2,1,0:T(8,128)(2,1)S(1)} copy-done((bf16[1,8,32,128]{3,2,1,0:T(8,128)(2,1)S(1)}, bf16[1,8,32,128]{3,2,1,0:T(8,128)(2,1)}, u32[]{:S(2)}) %copy-start) | copy-done | bytes 65560
  2.8 0.0 copy-start.1
  2.8 0.8 %copy-done.1 = bf16[1,8,32,128]{3,2,1,0:T(8,128)(2,1)S(1)} copy-done((bf16[1,8,32,128]{3,2,1,0:T(8,128)(2,1)S(1)}, bf16[1,8,32,128]{3,2,1,0:T(8,128)(2,1)}, u32[]{:S(2)}) %copy-start.1) | copy-done | bytes 65560
  3.6 55.3 %shard_map.59 = (f32[3,2,32,64]{3,2,1,0:T(8,128)S(1)}, f32[1,8,32,128]{3,2,1,0:T(8,128)S(1)}) custom-call(bf16[1,8,32,128]{3,2,1,0:T(8,128)(2,1)S(1)} %copy-done, bf16[1,8,32,128]{3,2,1,0:T(8,128)(2,1)S(1)} %copy-done.1, s32[1]{0:T(128)S(6)} %copy.8.place_ref, s32[1]{0:T(128)S(6)} %copy.9.tissue_ref), custom_call_target="tpu_custom_call" | custom-call | tf_op jit(solution)/shard_map/pallas_call | solution.py:392
  58.9 0.6 %copy.10 = f32[3,2,32,64]{3,2,1,0:T(8,128)} copy(f32[3,2,32,64]{3,2,1,0:T(8,128)S(1)} %get-tuple-element.4) | data formatting | bytes 98304
  59.6 0.7 %copy.11 = f32[1,8,32,128]{3,2,1,0:T(8,128)} copy(f32[1,8,32,128]{3,2,1,0:T(8,128)S(1)} %get-tuple-element.5) | data formatting | bytes 262144
Async XLA Ops:
  1.9 0.8 %copy-start = (bf16[1,8,32,128]{3,2,1,0:T(8,128)(2,1)S(1)}, bf16[1,8,32,128]{3,2,1,0:T(8,128)(2,1)}, u32[]{:S(2)}) copy-start(bf16[1,8,32,128]{3,2,1,0:T(8,128)(2,1)} %fixed_hbm.1) | copy-start | bytes 196612
  2.8 0.8 %copy-start.1 = (bf16[1,8,32,128]{3,2,1,0:T(8,128)(2,1)S(1)}, bf16[1,8,32,128]{3,2,1,0:T(8,128)(2,1)}, u32[]{:S(2)}) copy-start(bf16[1,8,32,128]{3,2,1,0:T(8,128)(2,1)} %moving_hbm.1) | copy-start | bytes 196612

commit v2 on v1

v2 whole, which is shorter than its diff:
```python
import functools
import math

import jax
import jax.numpy as jnp
from jax import lax
from jax.experimental import pallas as pl
from jax.experimental.pallas import tpu as pltpu
from jax.sharding import PartitionSpec as P

NX, NY, NZC = 4, 4, 16
F32, BF16 = jnp.float32, jnp.bfloat16
EPSILON = 1e-05
STEP_LENGTH = 0.5
RAW = [math.exp(-(t * t) / 4.5) for t in range(4)]
TOTAL = RAW[0] + 2 * (RAW[1] + RAW[2] + RAW[3])
W1, W2, W3 = (RAW[t] / TOTAL for t in (1, 2, 3))
PLACE_LANE = 48
MESH = pl.DeviceIdType.MESH


def coordinates():
    blk = lax.axis_index("blk")
    return blk // (2 * NZC), lax.axis_index("gz"), (blk // 2) % NZC, blk % 2


def device(x, y, z, core):
    return ((x * NZC + z) * 2 + core, y)


def far_first():
    steps = [(z, x, c) for z in range(NZC) for x in range(NX) for c in range(2)][1:]
    return sorted(steps, key=lambda s: -(min(s[0], NZC - s[0]) + min(s[1], NX - s[1]) + 0.3 * s[2]))


def peers():
    x, y, z, core = coordinates()
    along_y = [device(x, (y + d) % NY, z, core) for d in range(1, NY)]
    along_x = [device((x + d // 2) % NX, y, z, (core + d) % 2) for d in range(1, 2 * NX)]
    along_z = {d: device(x, y, (z + d) % NZC, core) for d in (1, 2, 3, 6, 10, 13, 14, 15)}
    others = [
        device((x + dx) % NX, y, (z + dz) % NZC, (core + dc) % 2) for dz, dx, dc in far_first()
    ]
    return along_y, along_x, along_z, others


def iota(shape, dim):
    return lax.broadcasted_iota(jnp.int32, shape, dim)


def split(value):
    high = value.astype(BF16)
    return high, (value - high.astype(F32)).astype(BF16)


def group_weight(t):
    near = jnp.minimum(t, 15 - t)
    out = jnp.where(near >= 3, 1.0, 0.0)
    for at, value in (
        (2, 1 - W3),
        (1, 1 - W3 - W2),
        (0, 1 - W3 - W2 - W1),
        (-1, W1 + W2 + W3),
        (-2, W2 + W3),
        (-3, W3),
    ):
        out = jnp.where(near == at, value, out)
    return out


def hat_tri(where, mark):
    gap = where - mark
    hat = lambda d: jnp.maximum(0.0, 1.0 - jnp.abs(d))
    return 0.5 * hat(gap) + 0.25 * (hat(gap - 1.0) + hat(gap + 1.0))


def own_sums(a):
    mid = a[3] + a[4]
    out0 = (a[0] + a[1]) + (a[2] + mid)
    out1 = out0 + a[5]
    out2 = out1 + a[6]
    out3 = out2 + a[7]
    out7 = mid + (a[5] + (a[6] + a[7]))
    out6 = out7 + a[2]
    out5 = out6 + a[1]
    return [out0, out1, out2, out3, out3, out5, out6, out7]


def side_sums(low, high):
    out3 = low[3]
    out2 = low[2] + out3
    out1 = low[1] + out2
    out0 = low[0] + out1
    out4 = high[0]
    out5 = out4 + high[1]
    out6 = out5 + high[2]
    out7 = out6 + high[3]
    return [out0, out1, out2, out3, out4, out5, out6, out7]


def shifted(value, amount, dim):
    size = value.shape[dim]
    at = iota(value.shape, dim)
    edge = 0 if amount == 1 else size - 1
    return jnp.where(at == edge, 0.0, pltpu.roll(value, amount % size, dim))


def kernel(
    fixed_hbm, moving_hbm, place_ref, tissue_ref,
    velocity_ref, cc_hbm,
    own_i, own_j, halo_i, halo_j,
    image_i, image_j, slope_x, slope_y, warped_ref,
    box_rows, box_cols, grad_rows, grad_cols, gauss_cols, spread,
    inner_sums, sums, means, stat_i, cc_ref, expanded, cols_twice,
    rows_y, rows, local_sem, halo_send, halo_recv, gather_send, gather_recv, known,
):
    gz = lax.axis_index("gz")
    along_y, along_x, along_z, others = peers()
    near_z = [along_z[d] for d in (1, 2, 3, 13, 14, 15)]
    barrier = pltpu.get_barrier_semaphore()
    for peer in along_y + along_x + near_z:
        pl.semaphore_signal(barrier, inc=1, device_id=peer, device_id_type=MESH)
    load_j = pltpu.make_async_copy(moving_hbm.at[0], own_j, local_sem.at[0])
    load_i = pltpu.make_async_copy(fixed_hbm.at[0], own_i, local_sem.at[1])
    load_j.start()
    load_i.start()
    pl.semaphore_wait(barrier, len(along_y) + len(along_x) + len(near_z))

    up, down = along_y[0], along_y[2]
    halos = []
    for index, (source, target, peer) in enumerate(
        (
            (moving_hbm.at[0, 3:8], halo_j.at[0], up),
            (moving_hbm.at[0, 0:5], halo_j.at[1], down),
            (fixed_hbm.at[0, 4:8], halo_i.at[0], up),
            (fixed_hbm.at[0, 0:4], halo_i.at[1], down),
        )
    ):
        copy = pltpu.make_async_remote_copy(
            source, target, halo_send.at[index], halo_recv.at[index],
            device_id=peer, device_id_type=MESH,
        )
        copy.start()
        halos.append(copy)
    for peer in near_z:
        pl.semaphore_signal(known.at[0], inc=1, device_id=peer, device_id_type=MESH)

    r, c = iota((256, 256), 0), iota((256, 256), 1)
    same = (r >> 5) == (c >> 5)
    box_rows[...] = jnp.where(same & (jnp.abs(r - c) <= 4), 1.0, 0.0).astype(BF16)
    grad_rows[...] = jnp.where(
        same & (c - r == 1), 0.5, jnp.where(same & (r - c == 1), -0.5, 0.0)
    ).astype(BF16)
    r, c = iota((128, 128), 0), iota((128, 128), 1)
    band = jnp.where(jnp.abs(r - c) <= 4, 1.0, 0.0).astype(BF16)
    box_cols[0:128, :] = band
    box_cols[128:256, :] = band
    grad_cols[...] = jnp.where(r - c == 1, 0.5, jnp.where(c - r == 1, -0.5, 0.0)).astype(BF16)
    high, low = split(group_weight(r - 16 * (c & 7)))
    gauss_cols[0:128, :] = high
    gauss_cols[128:256, :] = high
    gauss_cols[256:384, :] = low

    inside_low = jnp.where(gz > 0, 1.0, 0.0)
    inside_high = jnp.where(gz < NY - 1, 1.0, 0.0)
    load_j.wait()
    load_i.wait()
    for p in range(8):
        image_i[4 + p] = own_i[p].astype(F32)
        image_j[5 + p] = own_j[p].astype(F32)
    flat = own_j[...].reshape(256, 128)
    slope_x[128:384, :] = jnp.dot(grad_rows[...], flat, preferred_element_type=F32)
    slope_y[128:384, :] = jnp.dot(flat, grad_cols[...], preferred_element_type=F32)

    def box_sums(slot):
        field = jnp.dot(box_rows[...], sums[slot], preferred_element_type=F32)
        high, low = split(field[:, :128] + field[:, 128:])
        field = jnp.dot(
            jnp.concatenate([high, low], axis=1), box_cols[...], preferred_element_type=F32
        )
        return field * (1.0 / 729.0)

    def products(fixed, moved):
        return (
            fixed,
            [a * a for a in fixed],
            moved,
            [b * b for b in moved],
            [a * b for a, b in zip(fixed, moved)],
        )

    def put_sums(slot, chunk, inner, outer):
        for p in range(8):
            high, low = split(inner[p] + outer[p])
            at = pl.ds(32 * p + 16 * chunk, 16)
            sums[slot, at, 0:128] = high
            sums[slot, at, 128:256] = low

    for chunk in range(2):
        at = pl.ds(16 * chunk, 16)
        fixed = [image_i[4 + p, at, :] for p in range(8)]
        moved = [image_j[5 + p, at, :] for p in range(8)]
        for slot, planes in enumerate(products(fixed, moved)):
            for p, value in enumerate(own_sums(planes)):
                inner_sums[slot, p, at, :] = value

    for copy in halos:
        copy.wait_recv()
    pl.semaphore_wait(known.at[0], len(near_z))
    for d in (6, 10):
        pl.semaphore_signal(known.at[1], inc=1, device_id=along_z[d], device_id_type=MESH)

    for p in range(5):
        image_j[p] = halo_j[0, p].astype(F32) * inside_low
        image_j[13 + p] = halo_j[1, p].astype(F32) * inside_high
    for p in range(4):
        image_i[p] = halo_i[0, p].astype(F32) * inside_low
        image_i[12 + p] = halo_i[1, p].astype(F32) * inside_high

    depth_weight = []
    for p in range(8):
        at = gz * 8 + p
        first = group_weight(at)
        second = group_weight(at - 16)
        depth_weight.append((0.5 * first + 0.25 * second, 0.25 * first + 0.5 * second))
    lane = iota((32, 128), 1)
    lane_group = (lane >> 3) & 7
    row_weight = group_weight(iota((32, 128), 0) - 16 * (lane >> 6))
    place = place_ref[0]
    tissue = tissue_ref[0].astype(F32)

    def piece(planes, first):
        totals = [None] * 6
        for p in range(8):
            at = pl.ds(32 * p, 32)
            mean_i, var_i = stat_i[0, at, :], stat_i[1, at, :]
            mean_w = means[0, at, :]
            var_w = means[1, at, :] - mean_w * mean_w
            cov = means[2, at, :] - mean_i * mean_w
            denom = var_i * var_w + EPSILON
            ratio = cov / denom
            if not first:
                cc_ref[p] = cov * ratio
            image = image_i[4 + p]
            mid = planes[4 + p]
            dcc = 2.0 * ratio * (image - mean_i - cov / (var_w + EPSILON) * (mid - mean_w))
            if first:
                along_rows = slope_x[128 + 32 * p : 160 + 32 * p, :]
                along_cols = slope_y[128 + 32 * p : 160 + 32 * p, :]
            else:
                along_rows = 0.5 * (shifted(mid, -1, 0) - shifted(mid, 1, 0))
                along_cols = 0.5 * (shifted(mid, -1, 1) - shifted(mid, 1, 1))
            along_depth = 0.5 * (planes[5 + p] - planes[3 + p])
            for c, slope in enumerate((along_depth, along_rows, along_cols)):
                force = dcc * slope
                for k in range(2):
                    term = depth_weight[p][k] * force
                    totals[2 * c + k] = term if p == 0 else totals[2 * c + k] + term
        stack = []
        for ck in range(6):
            high, low = split(totals[ck])
            stack.append(jnp.concatenate([high, low, high], axis=1))
        parts = jnp.dot(
            jnp.concatenate(stack, axis=0), gauss_cols[...], preferred_element_type=F32
        )
        merged = jnp.zeros((32, 128), F32)
        for ck in range(6):
            merged = jnp.where(lane_group == ck, parts[32 * ck : 32 * ck + 32], merged)
        row = jnp.sum(merged * row_weight, axis=0, keepdims=True) * tissue
        lane_row = iota((1, 128), 1)
        return jnp.where(lane_row == PLACE_LANE, place.astype(F32) * 0.25, row)

    def exchange(source, targets, everything, sem, partners):
        for d, peer in enumerate(partners):
            pltpu.make_async_remote_copy(
                source, targets.at[d + 1], gather_send.at[sem], gather_recv.at[sem],
                device_id=peer, device_id_type=MESH,
            ).start()
        return pltpu.make_async_remote_copy(
            everything, everything, gather_send.at[sem], gather_recv.at[sem],
            device_id=partners[0], device_id_type=MESH,
        )

    def start_gather(turn, row):
        mine, every = rows_y.at[turn], rows.at[turn]
        rows_y[turn, 0] = row
        done_y = exchange(mine.at[0], mine, mine.at[1:NY], 2 * turn, along_y)
        if turn == 0:
            pl.semaphore_wait(known.at[1], 2)
        done_y.wait_recv()
        rows[turn, 0] = (rows_y[turn, 0] + rows_y[turn, 2]) + (rows_y[turn, 1] + rows_y[turn, 3])
        return done_y, exchange(every.at[0], every, every.at[1:128], 2 * turn + 1, others)

    for chunk in range(2):
        at = pl.ds(16 * chunk, 16)
        fixed = [image_i[p, at, :] for p in (0, 1, 2, 3, 12, 13, 14, 15)]
        moved = [image_j[1 + p, at, :] for p in (0, 1, 2, 3, 12, 13, 14, 15)]
        for slot, planes in enumerate(products(fixed, moved)):
            inner = [inner_sums[slot, p, at, :] for p in range(8)]
            put_sums(slot, chunk, inner, side_sums(planes[:4], planes[4:]))
    mean_i = box_sums(0)
    stat_i[0] = mean_i
    stat_i[1] = box_sums(1) - mean_i * mean_i
    for slot in range(3):
        means[slot] = box_sums(2 + slot)
    row = piece([image_j[1 + p] for p in range(16)], True)
    first_y, first = start_gather(0, row)

    r, c = iota((128, 768), 0), iota((128, 768), 1)
    half = jnp.where(c >= 384, 1, 0)
    c = c - 384 * half
    pick = ((r >> 6) == half) & (((r >> 3) & 7) == (c >> 6)) & ((r & 7) == (c & 7))
    pick = jnp.where(pick, 1.0, 0.0).astype(BF16)
    spread[0:128, :] = pick
    spread[128:256, :] = pick
    own_row, own_col = place >> 3, place & 7
    r, c = iota((128, 256), 0), iota((128, 256), 1)
    inner = (own_col * 128 + (c & 127)).astype(F32)
    inner = jnp.clip((inner + 0.5) * (1.0 / 16.0) - 0.5, 0.0, 63.0)
    to_cols = jnp.where(
        (r >> 6) == (c >> 7), hat_tri(inner, (r & 63).astype(F32)), 0.0
    ).astype(BF16)
    cols_twice[0:128, :] = to_cols
    cols_twice[128:256, :] = to_cols
    for start, side, offset in ((0, 0, 1), (384, 1, 0)):
        flat = halo_j[side, offset : offset + 4].reshape(128, 128)
        slope_x[start : start + 128, :] = jnp.dot(
            grad_rows[0:128, 0:128], flat, preferred_element_type=F32
        )
        slope_y[start : start + 128, :] = jnp.dot(
            flat, grad_cols[...], preferred_element_type=F32
        )

    first.wait_recv()
    gathered = rows[0].reshape(128, 128)

    spot = jnp.broadcast_to(gathered[:, PLACE_LANE : PLACE_LANE + 1], (128, 128)).astype(jnp.int32)
    r, c = iota((128, 128), 0), iota((128, 128), 1)
    in_column = (spot & 7) == ((c >> 3) & 7)
    spot_row = jnp.sum(jnp.where(r == c, spot, 0).astype(F32), axis=0, keepdims=True).astype(
        jnp.int32
    )
    mark = ((spot_row >> 3) * 2).astype(F32)
    mark = jnp.broadcast_to(jnp.concatenate([mark, mark + 1.0], axis=1), (64, 256))
    at = iota((64, 256), 0)
    inner = (own_row * 32 + at - 32).astype(F32)
    inner = jnp.clip((inner + 0.5) * (1.0 / 16.0) - 0.5, 0.0, 31.0)
    where = jnp.where(at < 32, at.astype(F32), inner)
    combine = hat_tri(where, mark).astype(BF16)
    combine = jnp.concatenate([combine, combine], axis=1)

    def grid_of(gathered, count):
        high, low = split(gathered)
        wide = jnp.dot(
            jnp.concatenate([high, low], axis=1), spread[...], preferred_element_type=F32
        )
        for tile in range(6):
            value = jnp.where(in_column, wide[:, 128 * tile : 128 * tile + 128], 0.0)
            high, low = split(value)
            at = 128 * (tile // 3)
            lanes = pl.ds(128 * (tile % 3), 128)
            expanded[at : at + 128, lanes] = high
            expanded[256 + at : 384 + at, lanes] = low
        return jnp.dot(combine[0:count], expanded[...], preferred_element_type=F32)

    def regular_of(grid):
        out = []
        at = iota((32, 128), 1) & 63
        squares = jnp.zeros((32, 128), F32)
        for tile in range(3):
            value = grid[:, 128 * tile : 128 * tile + 128]
            left = jnp.where(at == 0, 0.0, pltpu.roll(value, 1, 1))
            right = jnp.where(at == 63, 0.0, pltpu.roll(value, 127, 1))
            value = 0.5 * value + 0.25 * (left + right)
            squares = squares + value * value
            out.append(value)
        mean = jnp.sum(squares, keepdims=True) * (1.0 / (6 * 32 * 64))
        return out, STEP_LENGTH / jnp.sqrt(mean + EPSILON)

    grid = grid_of(gathered, 64)
    regular, scale = regular_of(grid[0:32])
    before = [value * scale for value in regular]
    stack = []
    for tile in range(3):
        stack.append(
            jnp.concatenate(split(grid[32:64, 128 * tile : 128 * tile + 128]), axis=1)
        )
    moves = scale * jnp.dot(
        jnp.concatenate(stack, axis=0), cols_twice[...], preferred_element_type=F32
    )
    shift = []
    for c in range(3):
        value = moves[32 * c : 32 * c + 32]
        shift.append((value[:, :128], value[:, 128:] - value[:, :128]))

    for p in range(16):
        deep = (gz * 8 + (p - 4)).astype(F32)
        part = jnp.clip((deep + 0.5) * (1.0 / 16.0) - 0.5, 0.0, 1.0)
        value = image_j[1 + p]
        slopes = (
            0.5 * (image_j[2 + p] - image_j[p]),
            slope_x[32 * p : 32 * p + 32, :],
            slope_y[32 * p : 32 * p + 32, :],
        )
        for (base, rise), slope in zip(shift, slopes):
            value = value + (base + part * rise) * slope
        if p < 4:
            value = value * inside_low
        if p >= 12:
            value = value * inside_high
        warped_ref[p] = value
    for chunk in range(2):
        at = pl.ds(16 * chunk, 16)
        fixed = [image_i[p, at, :] for p in range(16)]
        moved = [warped_ref[p, at, :] for p in range(16)]
        for slot, planes in enumerate(products(fixed, moved)):
            if slot >= 2:
                put_sums(
                    slot, chunk, own_sums(planes[4:12]), side_sums(planes[0:4], planes[12:16])
                )
    for slot in range(3):
        means[slot] = box_sums(2 + slot)
    row = piece([warped_ref[p] for p in range(16)], False)
    store = pltpu.make_async_copy(cc_ref, cc_hbm.at[0], local_sem.at[0])
    store.start()
    second_y, second = start_gather(1, row)
    second.wait_recv()
    regular, scale = regular_of(grid_of(rows[1].reshape(128, 128), 32))
    for tile in range(3):
        value = before[tile] + regular[tile] * scale
        velocity_ref[tile, 0] = value[:, 0:64]
        velocity_ref[tile, 1] = value[:, 64:128]
    for copy in halos:
        copy.wait_send()
    for copy in (first_y, first, second_y, second):
        copy.wait_send()
    store.wait()


def per_device(fixed, moving, block_place, tissue):
    vmem = pltpu.VMEM
    return pl.pallas_call(
        kernel,
        out_shape=(
            jax.ShapeDtypeStruct((3, 2, 32, 64), F32),
            jax.ShapeDtypeStruct((1, 8, 32, 128), F32),
        ),
        in_specs=[
            pl.BlockSpec(memory_space=pltpu.HBM),
            pl.BlockSpec(memory_space=pltpu.HBM),
            pl.BlockSpec(memory_space=pltpu.SMEM),
            pl.BlockSpec(memory_space=pltpu.SMEM),
        ],
        out_specs=(
            pl.BlockSpec(memory_space=pltpu.VMEM),
            pl.BlockSpec(memory_space=pl.ANY),
        ),
        scratch_shapes=[
            vmem((8, 32, 128), BF16),
            vmem((8, 32, 128), BF16),
            vmem((2, 4, 32, 128), BF16),
            vmem((2, 5, 32, 128), BF16),
            vmem((16, 32, 128), F32),
            vmem((18, 32, 128), F32),
            vmem((512, 128), F32),
            vmem((512, 128), F32),
            vmem((16, 32, 128), F32),
            vmem((256, 256), BF16),
            vmem((256, 128), BF16),
            vmem((256, 256), BF16),
            vmem((128, 128), BF16),
            vmem((384, 128), BF16),
            vmem((256, 768), BF16),
            vmem((5, 8, 32, 128), F32),
            vmem((5, 256, 256), BF16),
            vmem((3, 256, 128), F32),
            vmem((2, 256, 128), F32),
            vmem((8, 32, 128), F32),
            vmem((512, 384), BF16),
            vmem((256, 256), BF16),
            vmem((2, NY, 1, 128), F32),
            vmem((2, 128, 1, 128), F32),
            pltpu.SemaphoreType.DMA((2,)),
            pltpu.SemaphoreType.DMA((4,)),
            pltpu.SemaphoreType.DMA((4,)),
            pltpu.SemaphoreType.DMA((4,)),
            pltpu.SemaphoreType.DMA((4,)),
            pltpu.SemaphoreType.REGULAR((2,)),
        ],
        compiler_params=pltpu.CompilerParams(
            collective_id=0, has_side_effects=True, vmem_limit_bytes=32 * 1024 * 1024
        ),
    )(
        pltpu.with_memory_space_constraint(fixed, pltpu.HBM),
        pltpu.with_memory_space_constraint(moving, pltpu.HBM),
        block_place,
        tissue,
    )


def solution(mesh):
    return jax.shard_map(
        per_device,
        mesh=mesh,
        in_specs=(P("blk", "gz", None, None), P("blk", "gz", None, None), P("blk"), P("blk")),
        out_specs=(P(), P("blk", "gz", None, None)),
        check_vma=False,
    )
```

time: 60.5 us -> 50.7 us (0.84)
  Pallas kernels: 55.3 us -> 47.3 us
  local copies, waits for them, and re-layouts: 2.97 us -> 1.3 us
    pallas_call x1, Pallas kernels: 55.3 us -> 47.3 us  [per_device(): pl.pallas_call(kernel, out_shape=(jax.ShapeDtypeStruct((3, 2, 32, 64), F3...]
    unnamed x6 -> x2, local copies, waits for them, and re-layouts: 2.97 us -> 1.3 us
where the time goes in v2:
time: 50.7 us; the launch traced here: 50.6 us
  Pallas kernels  47.3 us (93%)
  between operations  1.93 us (4%)
  local copies, waits for them, and re-layouts  1.3 us (3%)
    pallas_call x1, Pallas kernels, per_device(): pl.pallas_call(kernel, out_shape=(jax.ShapeDtypeStruct((3, 2, 32, 64), F3...  47.3 us
    unnamed x2, local copies, waits for them, and re-layouts  1.3 us

profile of v2, /device:TPU:1, one launch (start us, length us, event | category | flops | bytes accessed | tf_op | source)
XLA Modules:
  0.0 50.6 jit_solution(13991287291790069577)
XLA Ops:
  1.9 47.3 %shard_map.59 = (f32[3,2,32,64]{3,2,1,0:T(8,128)S(1)}, f32[1,8,32,128]{3,2,1,0:T(8,128)S(1)}) custom-call(bf16[1,8,32,128]{3,2,1,0:T(8,128)(2,1)} %fixed_hbm.1, bf16[1,8,32,128]{3,2,1,0:T(8,128)(2,1)} %moving_hbm.1, s32[1]{0:T(128)S(6)} %copy.8.place_ref, s32[1]{0:T(128)S(6)} %copy.9.tissue_ref), custom_call_target="tpu_custom_call" | custom-call | tf_op jit(solution)/shard_map/pallas_call | solution.py:442
  49.3 0.6 %copy.10 = f32[3,2,32,64]{3,2,1,0:T(8,128)} copy(f32[3,2,32,64]{3,2,1,0:T(8,128)S(1)} %get-tuple-element.4) | data formatting | bytes 98304
  49.9 0.7 %copy.11 = f32[1,8,32,128]{3,2,1,0:T(8,128)} copy(f32[1,8,32,128]{3,2,1,0:T(8,128)S(1)} %get-tuple-element.5) | data formatting | bytes 262144

commit v3 on v2

--- a/solution.py
+++ b/solution.py
@@ -15,7 +15,8 @@
 RAW = [math.exp(-(t * t) / 4.5) for t in range(4)]
 TOTAL = RAW[0] + 2 * (RAW[1] + RAW[2] + RAW[3])
 W1, W2, W3 = (RAW[t] / TOTAL for t in (1, 2, 3))
-PLACE_LANE = 48
+WIDE = 10
+PLACE_LANE = 60
 MESH = pl.DeviceIdType.MESH
 
 
@@ -46,6 +47,12 @@
 
 def iota(shape, dim):
     return lax.broadcasted_iota(jnp.int32, shape, dim)
+
+
+def lane_parts(shape):
+    lane = iota(shape, len(shape) - 1) & 63
+    group = (lane * 205) >> 11
+    return group, lane - WIDE * group
 
 
 def split(value):
@@ -110,8 +117,8 @@
     velocity_ref, cc_hbm,
     own_i, own_j, halo_i, halo_j,
     image_i, image_j, slope_x, slope_y, warped_ref,
-    box_rows, box_cols, grad_rows, grad_cols, gauss_cols, spread,
-    inner_sums, sums, means, stat_i, cc_ref, expanded, cols_twice,
+    box_rows, box_cols, grad_rows, grad_cols, gauss_cols, to_cols,
+    inner_sums, sums, means, stat_i, cc_ref, combine, before,
     rows_y, rows, local_sem, halo_send, halo_recv, gather_send, gather_recv, known,
 ):
     gz = lax.axis_index("gz")
@@ -130,10 +137,12 @@
     halos = []
     for index, (source, target, peer) in enumerate(
         (
-            (moving_hbm.at[0, 3:8], halo_j.at[0], up),
-            (moving_hbm.at[0, 0:5], halo_j.at[1], down),
+            (moving_hbm.at[0, 4:8], halo_j.at[0, 1:5], up),
+            (moving_hbm.at[0, 0:4], halo_j.at[1, 0:4], down),
             (fixed_hbm.at[0, 4:8], halo_i.at[0], up),
             (fixed_hbm.at[0, 0:4], halo_i.at[1], down),
+            (moving_hbm.at[0, 3:4], halo_j.at[0, 0:1], up),
+            (moving_hbm.at[0, 4:5], halo_j.at[1, 4:5], down),
         )
     ):
         copy = pltpu.make_async_remote_copy(
@@ -156,7 +165,12 @@
     box_cols[0:128, :] = band
     box_cols[128:256, :] = band
     grad_cols[...] = jnp.where(r - c == 1, 0.5, jnp.where(c - r == 1, -0.5, 0.0)).astype(BF16)
-    high, low = split(group_weight(r - 16 * (c & 7)))
+    turn = lane_parts((128, 128))[1] - 1
+    weight = jnp.zeros((128, 128), F32)
+    for step, share in ((-1, 0.25), (0, 0.5), (1, 0.25)):
+        b = turn + step
+        weight = weight + jnp.where((b >= 0) & (b < 8), share * group_weight(r - 16 * b), 0.0)
+    high, low = split(weight)
     gauss_cols[0:128, :] = high
     gauss_cols[128:256, :] = high
     gauss_cols[256:384, :] = low
@@ -204,16 +218,15 @@
             for p, value in enumerate(own_sums(planes)):
                 inner_sums[slot, p, at, :] = value
 
-    for copy in halos:
-        copy.wait_recv()
     pl.semaphore_wait(known.at[0], len(near_z))
     for d in (6, 10):
         pl.semaphore_signal(known.at[1], inc=1, device_id=along_z[d], device_id_type=MESH)
 
-    for p in range(5):
-        image_j[p] = halo_j[0, p].astype(F32) * inside_low
+    for copy in halos[:4]:
+        copy.wait_recv()
+    for p in range(4):
+        image_j[1 + p] = halo_j[0, 1 + p].astype(F32) * inside_low
         image_j[13 + p] = halo_j[1, p].astype(F32) * inside_high
-    for p in range(4):
         image_i[p] = halo_i[0, p].astype(F32) * inside_low
         image_i[12 + p] = halo_i[1, p].astype(F32) * inside_high
 
@@ -224,7 +237,7 @@
         second = group_weight(at - 16)
         depth_weight.append((0.5 * first + 0.25 * second, 0.25 * first + 0.5 * second))
     lane = iota((32, 128), 1)
-    lane_group = (lane >> 3) & 7
+    lane_group, lane_turn = lane_parts((32, 128))
     row_weight = group_weight(iota((32, 128), 0) - 16 * (lane >> 6))
     place = place_ref[0]
     tissue = tissue_ref[0].astype(F32)
@@ -306,22 +319,22 @@
     row = piece([image_j[1 + p] for p in range(16)], True)
     first_y, first = start_gather(0, row)
 
-    r, c = iota((128, 768), 0), iota((128, 768), 1)
-    half = jnp.where(c >= 384, 1, 0)
-    c = c - 384 * half
-    pick = ((r >> 6) == half) & (((r >> 3) & 7) == (c >> 6)) & ((r & 7) == (c & 7))
-    pick = jnp.where(pick, 1.0, 0.0).astype(BF16)
-    spread[0:128, :] = pick
-    spread[128:256, :] = pick
     own_row, own_col = place >> 3, place & 7
-    r, c = iota((128, 256), 0), iota((128, 256), 1)
-    inner = (own_col * 128 + (c & 127)).astype(F32)
+    r, c = iota((128, 128), 0), iota((128, 128), 1)
+    inner = (own_col * 128 + c).astype(F32)
     inner = jnp.clip((inner + 0.5) * (1.0 / 16.0) - 0.5, 0.0, 63.0)
-    to_cols = jnp.where(
-        (r >> 6) == (c >> 7), hat_tri(inner, (r & 63).astype(F32)), 0.0
-    ).astype(BF16)
-    cols_twice[0:128, :] = to_cols
-    cols_twice[128:256, :] = to_cols
+    turn = (r & 63) - WIDE * (((r & 63) * 205) >> 11) - 1
+    for first_row, col in ((0, own_col - jnp.where(r < 64, 1, 0)), (256, own_col + 1)):
+        gap = inner - (8 * col + turn).astype(F32)
+        weight = jnp.maximum(0.0, 1.0 - jnp.abs(gap)).astype(BF16)
+        to_cols[first_row : first_row + 128, :] = weight
+        if first_row == 0:
+            to_cols[128:256, :] = weight
+
+    for copy in halos[4:]:
+        copy.wait_recv()
+    image_j[0] = halo_j[0, 0].astype(F32) * inside_low
+    image_j[17] = halo_j[1, 4].astype(F32) * inside_high
     for start, side, offset in ((0, 0, 1), (384, 1, 0)):
         flat = halo_j[side, offset : offset + 4].reshape(128, 128)
         slope_x[start : start + 128, :] = jnp.dot(
@@ -334,64 +347,68 @@
     first.wait_recv()
     gathered = rows[0].reshape(128, 128)
 
-    spot = jnp.broadcast_to(gathered[:, PLACE_LANE : PLACE_LANE + 1], (128, 128)).astype(jnp.int32)
+    spot = jnp.broadcast_to(gathered[:, PLACE_LANE : PLACE_LANE + 1], (128, 128))
     r, c = iota((128, 128), 0), iota((128, 128), 1)
-    in_column = (spot & 7) == ((c >> 3) & 7)
-    spot_row = jnp.sum(jnp.where(r == c, spot, 0).astype(F32), axis=0, keepdims=True).astype(
-        jnp.int32
-    )
-    mark = ((spot_row >> 3) * 2).astype(F32)
-    mark = jnp.broadcast_to(jnp.concatenate([mark, mark + 1.0], axis=1), (64, 256))
-    at = iota((64, 256), 0)
-    inner = (own_row * 32 + at - 32).astype(F32)
-    inner = jnp.clip((inner + 0.5) * (1.0 / 16.0) - 0.5, 0.0, 31.0)
-    where = jnp.where(at < 32, at.astype(F32), inner)
-    combine = hat_tri(where, mark).astype(BF16)
-    combine = jnp.concatenate([combine, combine], axis=1)
-
-    def grid_of(gathered, count):
-        high, low = split(gathered)
-        wide = jnp.dot(
-            jnp.concatenate([high, low], axis=1), spread[...], preferred_element_type=F32
-        )
-        for tile in range(6):
-            value = jnp.where(in_column, wide[:, 128 * tile : 128 * tile + 128], 0.0)
-            high, low = split(value)
-            at = 128 * (tile // 3)
-            lanes = pl.ds(128 * (tile % 3), 128)
-            expanded[at : at + 128, lanes] = high
-            expanded[256 + at : 384 + at, lanes] = low
-        return jnp.dot(combine[0:count], expanded[...], preferred_element_type=F32)
+    spot = jnp.sum(jnp.where(r == c, spot, 0.0), axis=0, keepdims=True).astype(jnp.int32)
+    mark = ((spot >> 3) * 2).astype(F32)
+    mark = jnp.broadcast_to(jnp.concatenate([mark, mark + 1.0], axis=1), (32, 256))
+    spot_col = jnp.broadcast_to(jnp.concatenate([spot & 7, spot & 7], axis=1), (32, 256))
+    at = iota((32, 256), 0)
+    filtered = hat_tri(at.astype(F32), mark)
+    inner = (own_row * 32 + at).astype(F32)
+    inner = hat_tri(jnp.clip((inner + 0.5) * (1.0 / 16.0) - 0.5, 0.0, 31.0), mark)
+    for d in range(3):
+        value = jnp.where(spot_col == own_col + (d - 1), inner, 0.0)
+        combine[32 * d : 32 * d + 32, :] = value.astype(BF16)
+    for col in range(8):
+        value = jnp.where(spot_col == col, filtered, 0.0)
+        combine[96 + 32 * col : 128 + 32 * col, :] = value.astype(BF16)
+
+    first_half = iota((128, 128), 1) < 64
+    groups, turns = lane_parts((32, 128))
+
+    def combined(gathered, start):
+        turned = pltpu.roll(gathered, 64, 1)
+        right = lambda high, low: jnp.where(first_half, high, low - low.astype(BF16).astype(F32))
+        both = jnp.concatenate([right(gathered, turned), right(turned, gathered)], axis=0)
+        value = jnp.dot(combine[start:352, :], both.astype(BF16), preferred_element_type=F32)
+        return value + pltpu.roll(value, 64, 1)
 
     def regular_of(grid):
+        cols = [grid[32 * col : 32 * col + 32] for col in range(8)]
         out = []
-        at = iota((32, 128), 1) & 63
         squares = jnp.zeros((32, 128), F32)
-        for tile in range(3):
-            value = grid[:, 128 * tile : 128 * tile + 128]
-            left = jnp.where(at == 0, 0.0, pltpu.roll(value, 1, 1))
-            right = jnp.where(at == 63, 0.0, pltpu.roll(value, 127, 1))
-            value = 0.5 * value + 0.25 * (left + right)
+        inside = (turns >= 1) & (turns <= 8) & (groups < 6) & (iota((32, 128), 1) < 64)
+        for col in range(8):
+            value = cols[col]
+            if col > 0:
+                value = value + jnp.where(turns == 1, pltpu.roll(cols[col - 1], 120, 1), 0.0)
+            if col < 7:
+                value = value + jnp.where(turns == 8, pltpu.roll(cols[col + 1], 8, 1), 0.0)
+            value = jnp.where(inside, value, 0.0)
             squares = squares + value * value
             out.append(value)
         mean = jnp.sum(squares, keepdims=True) * (1.0 / (6 * 32 * 64))
         return out, STEP_LENGTH / jnp.sqrt(mean + EPSILON)
 
-    grid = grid_of(gathered, 64)
-    regular, scale = regular_of(grid[0:32])
-    before = [value * scale for value in regular]
-    stack = []
-    for tile in range(3):
-        stack.append(
-            jnp.concatenate(split(grid[32:64, 128 * tile : 128 * tile + 128]), axis=1)
-        )
-    moves = scale * jnp.dot(
-        jnp.concatenate(stack, axis=0), cols_twice[...], preferred_element_type=F32
-    )
+    grid = combined(gathered, 0)
+    half = first_half[0:32]
+    near = jnp.where(half, grid[0:32], grid[32:64])
+    high, low = split(near)
+    above_high, above_low = split(grid[64:96])
+    above = jnp.where(half, above_high.astype(F32), above_low.astype(F32)).astype(BF16)
+    wide = jnp.concatenate([high, low, above], axis=1)
+    group_wide = jnp.concatenate([groups, groups, groups], axis=1)
+    stack = [jnp.where(group_wide == ck, wide, jnp.zeros_like(wide)) for ck in range(6)]
+    moves = jnp.dot(jnp.concatenate(stack, axis=0), to_cols[...], preferred_element_type=F32)
+    regular, scale = regular_of(grid[96:352])
+    for col in range(8):
+        before[col] = regular[col] * scale
+    moves = moves * scale
     shift = []
     for c in range(3):
-        value = moves[32 * c : 32 * c + 32]
-        shift.append((value[:, :128], value[:, 128:] - value[:, :128]))
+        value, other = moves[64 * c : 64 * c + 32], moves[64 * c + 32 : 64 * c + 64]
+        shift.append((value, other - value))
 
     for p in range(16):
         deep = (gz * 8 + (p - 4)).astype(F32)
@@ -425,11 +442,15 @@
     store.start()
     second_y, second = start_gather(1, row)
     second.wait_recv()
-    regular, scale = regular_of(grid_of(rows[1].reshape(128, 128), 32))
-    for tile in range(3):
-        value = before[tile] + regular[tile] * scale
-        velocity_ref[tile, 0] = value[:, 0:64]
-        velocity_ref[tile, 1] = value[:, 64:128]
+    regular, scale = regular_of(combined(rows[1].reshape(128, 128), 96))
+    total = [before[col] + regular[col] * scale for col in range(8)]
+    lane_col = iota((32, 128), 1) >> 3
+    for ck in range(6):
+        value = jnp.zeros((32, 128), F32)
+        for col in range(8):
+            moved = pltpu.roll(total[col], (8 * col - WIDE * ck - 1) % 128, 1)
+            value = jnp.where(lane_col == col, moved, value)
+        velocity_ref[ck // 2, ck % 2] = value[:, 0:64]
     for copy in halos:
         copy.wait_send()
     for copy in (first_y, first, second_y, second):
@@ -470,19 +491,19 @@
             vmem((256, 256), BF16),
             vmem((128, 128), BF16),
             vmem((384, 128), BF16),
-            vmem((256, 768), BF16),
+            vmem((384, 128), BF16),
             vmem((5, 8, 32, 128), F32),
             vmem((5, 256, 256), BF16),
             vmem((3, 256, 128), F32),
             vmem((2, 256, 128), F32),
             vmem((8, 32, 128), F32),
-            vmem((512, 384), BF16),
-            vmem((256, 256), BF16),
+            vmem((352, 256), BF16),
+            vmem((8, 32, 128), F32),
             vmem((2, NY, 1, 128), F32),
             vmem((2, 128, 1, 128), F32),
             pltpu.SemaphoreType.DMA((2,)),
-            pltpu.SemaphoreType.DMA((4,)),
-            pltpu.SemaphoreType.DMA((4,)),
+            pltpu.SemaphoreType.DMA((6,)),
+            pltpu.SemaphoreType.DMA((6,)),
             pltpu.SemaphoreType.DMA((4,)),
             pltpu.SemaphoreType.DMA((4,)),
             pltpu.SemaphoreType.REGULAR((2,)),

time: 50.7 us -> 48.3 us (0.953)
  Pallas kernels: 47.3 us -> 45 us
    pallas_call x1, Pallas kernels: 47.3 us -> 45 us  [per_device(): pl.pallas_call(kernel, out_shape=(jax.ShapeDtypeStruct((3, 2, 32, 64), F3...]
where the time goes in v3:
time: 48.3 us; the launch traced here: 48.2 us
  Pallas kernels  45 us (93%)
  between operations  1.93 us (4%)
  local copies, waits for them, and re-layouts  1.3 us (3%)
    pallas_call x1, Pallas kernels, per_device(): pl.pallas_call(kernel, out_shape=(jax.ShapeDtypeStruct((3, 2, 32, 64), F3...  45 us
    unnamed x2, local copies, waits for them, and re-layouts  1.3 us

profile of v3, /device:TPU:1, one launch (start us, length us, event | category | flops | bytes accessed | tf_op | source)
XLA Modules:
  0.0 48.2 jit_solution(3372261400700830673)
XLA Ops:
  1.9 45.0 %shard_map.59 = (f32[3,2,32,64]{3,2,1,0:T(8,128)S(1)}, f32[1,8,32,128]{3,2,1,0:T(8,128)S(1)}) custom-call(bf16[1,8,32,128]{3,2,1,0:T(8,128)(2,1)} %fixed_hbm.1, bf16[1,8,32,128]{3,2,1,0:T(8,128)(2,1)} %moving_hbm.1, s32[1]{0:T(128)S(6)} %copy.8.place_ref, s32[1]{0:T(128)S(6)} %copy.9.tissue_ref), custom_call_target="tpu_custom_call" | custom-call | tf_op jit(solution)/shard_map/pallas_call | solution.py:463
  46.9 0.6 %copy.10 = f32[3,2,32,64]{3,2,1,0:T(8,128)} copy(f32[3,2,32,64]{3,2,1,0:T(8,128)S(1)} %get-tuple-element.4) | data formatting | bytes 98304
  47.6 0.7 %copy.11 = f32[1,8,32,128]{3,2,1,0:T(8,128)} copy(f32[1,8,32,128]{3,2,1,0:T(8,128)S(1)} %get-tuple-element.5) | data formatting | bytes 262144

commit v4 on v3

--- a/solution.py
+++ b/solution.py
@@ -18,6 +18,7 @@
 WIDE = 10
 PLACE_LANE = 60
 MESH = pl.DeviceIdType.MESH
+ROUNDS = (1, 2, 4, 1)
 
 
 def coordinates():
@@ -25,23 +26,21 @@
     return blk // (2 * NZC), lax.axis_index("gz"), (blk // 2) % NZC, blk % 2
 
 
-def device(x, y, z, core):
-    return ((x * NZC + z) * 2 + core, y)
-
-
 def far_first():
     steps = [(z, x, c) for z in range(NZC) for x in range(NX) for c in range(2)][1:]
-    return sorted(steps, key=lambda s: -(min(s[0], NZC - s[0]) + min(s[1], NX - s[1]) + 0.3 * s[2]))
+    return sorted(steps, key=lambda s: -(4 * min(s[0], NZC - s[0]) + min(s[1], NX - s[1]) + 0.3 * s[2]))
 
 
 def peers():
     x, y, z, core = coordinates()
-    along_y = [device(x, (y + d) % NY, z, core) for d in range(1, NY)]
-    along_x = [device((x + d // 2) % NX, y, z, (core + d) % 2) for d in range(1, 2 * NX)]
-    along_z = {d: device(x, y, (z + d) % NZC, core) for d in (1, 2, 3, 6, 10, 13, 14, 15)}
-    others = [
-        device((x + dx) % NX, y, (z + dz) % NZC, (core + dc) % 2) for dz, dx, dc in far_first()
-    ]
+    at_x = [(x + d) % NX * (2 * NZC) for d in range(NX)]
+    at_z = [(z + d) % NZC * 2 for d in range(NZC)]
+    at_core = [core, 1 - core]
+    base = x * (2 * NZC) + z * 2 + core
+    along_y = [(base, (y + d) % NY) for d in (2, 1, 3)]
+    along_x = [(at_x[d // 2] + at_z[0] + at_core[d % 2], y) for d in range(1, 2 * NX)]
+    along_z = {d: (at_x[0] + at_z[d % NZC] + core, y) for d in (1, 2, 4, -1, -2, -4)}
+    others = [(at_x[dx] + at_z[dz] + at_core[dc], y) for dz, dx, dc in far_first()]
     return along_y, along_x, along_z, others
 
 
@@ -113,34 +112,38 @@
 
 
 def kernel(
-    fixed_hbm, moving_hbm, place_ref, tissue_ref,
-    velocity_ref, cc_hbm,
+    fixed_hbm, moving_hbm, place_in, tissue_in,
+    velocity_ref, cc_ref,
     own_i, own_j, halo_i, halo_j,
     image_i, image_j, slope_x, slope_y, warped_ref,
     box_rows, box_cols, grad_rows, grad_cols, gauss_cols, to_cols,
-    inner_sums, sums, means, stat_i, cc_ref, combine, before,
-    rows_y, rows, local_sem, halo_send, halo_recv, gather_send, gather_recv, known,
+    inner_sums, sums, means, stat_i, combine, before,
+    rows_y, rows, place_ref, tissue_ref, local_sem, halo_send, halo_recv, gather_send, gather_recv, known,
 ):
     gz = lax.axis_index("gz")
     along_y, along_x, along_z, others = peers()
-    near_z = [along_z[d] for d in (1, 2, 3, 13, 14, 15)]
+    next_z = [along_z[1], along_z[-1]]
     barrier = pltpu.get_barrier_semaphore()
-    for peer in along_y + along_x + near_z:
+    for peer in along_y + along_x + next_z:
         pl.semaphore_signal(barrier, inc=1, device_id=peer, device_id_type=MESH)
     load_j = pltpu.make_async_copy(moving_hbm.at[0], own_j, local_sem.at[0])
     load_i = pltpu.make_async_copy(fixed_hbm.at[0], own_i, local_sem.at[1])
+    load_place = pltpu.make_async_copy(place_in, place_ref, local_sem.at[2])
+    load_tissue = pltpu.make_async_copy(tissue_in, tissue_ref, local_sem.at[3])
     load_j.start()
     load_i.start()
-    pl.semaphore_wait(barrier, len(along_y) + len(along_x) + len(near_z))
-
-    up, down = along_y[0], along_y[2]
+    load_place.start()
+    load_tissue.start()
+    pl.semaphore_wait(barrier, len(along_y) + len(along_x) + len(next_z))
+
+    up, down = along_y[1], along_y[2]
     halos = []
     for index, (source, target, peer) in enumerate(
         (
+            (fixed_hbm.at[0, 4:8], halo_i.at[0], up),
+            (fixed_hbm.at[0, 0:4], halo_i.at[1], down),
             (moving_hbm.at[0, 4:8], halo_j.at[0, 1:5], up),
             (moving_hbm.at[0, 0:4], halo_j.at[1, 0:4], down),
-            (fixed_hbm.at[0, 4:8], halo_i.at[0], up),
-            (fixed_hbm.at[0, 0:4], halo_i.at[1], down),
             (moving_hbm.at[0, 3:4], halo_j.at[0, 0:1], up),
             (moving_hbm.at[0, 4:5], halo_j.at[1, 4:5], down),
         )
@@ -151,8 +154,11 @@
         )
         copy.start()
         halos.append(copy)
-    for peer in near_z:
-        pl.semaphore_signal(known.at[0], inc=1, device_id=peer, device_id_type=MESH)
+    def tell(index):
+        for d in (ROUNDS[index], -ROUNDS[index]):
+            pl.semaphore_signal(known.at[index], inc=1, device_id=along_z[d], device_id_type=MESH)
+
+    tell(0)
 
     r, c = iota((256, 256), 0), iota((256, 256), 1)
     same = (r >> 5) == (c >> 5)
@@ -179,6 +185,8 @@
     inside_high = jnp.where(gz < NY - 1, 1.0, 0.0)
     load_j.wait()
     load_i.wait()
+    load_place.wait()
+    load_tissue.wait()
     for p in range(8):
         image_i[4 + p] = own_i[p].astype(F32)
         image_j[5 + p] = own_j[p].astype(F32)
@@ -218,15 +226,14 @@
             for p, value in enumerate(own_sums(planes)):
                 inner_sums[slot, p, at, :] = value
 
-    pl.semaphore_wait(known.at[0], len(near_z))
-    for d in (6, 10):
-        pl.semaphore_signal(known.at[1], inc=1, device_id=along_z[d], device_id_type=MESH)
-
-    for copy in halos[:4]:
+    pl.semaphore_wait(known.at[0], 2)
+    tell(1)
+    pl.semaphore_wait(known.at[1], 2)
+    tell(2)
+
+    for copy in halos[:2]:
         copy.wait_recv()
     for p in range(4):
-        image_j[1 + p] = halo_j[0, 1 + p].astype(F32) * inside_low
-        image_j[13 + p] = halo_j[1, p].astype(F32) * inside_high
         image_i[p] = halo_i[0, p].astype(F32) * inside_low
         image_i[12 + p] = halo_i[1, p].astype(F32) * inside_high
 
@@ -242,7 +249,7 @@
     place = place_ref[0]
     tissue = tissue_ref[0].astype(F32)
 
-    def piece(planes, first):
+    def piece(images, first):
         totals = [None] * 6
         for p in range(8):
             at = pl.ds(32 * p, 32)
@@ -253,9 +260,9 @@
             denom = var_i * var_w + EPSILON
             ratio = cov / denom
             if not first:
-                cc_ref[p] = cov * ratio
+                cc_ref[0, p] = cov * ratio
             image = image_i[4 + p]
-            mid = planes[4 + p]
+            mid = images[4 + p]
             dcc = 2.0 * ratio * (image - mean_i - cov / (var_w + EPSILON) * (mid - mean_w))
             if first:
                 along_rows = slope_x[128 + 32 * p : 160 + 32 * p, :]
@@ -263,7 +270,7 @@
             else:
                 along_rows = 0.5 * (shifted(mid, -1, 0) - shifted(mid, 1, 0))
                 along_cols = 0.5 * (shifted(mid, -1, 1) - shifted(mid, 1, 1))
-            along_depth = 0.5 * (planes[5 + p] - planes[3 + p])
+            along_depth = 0.5 * (images[5 + p] - images[3 + p])
             for c, slope in enumerate((along_depth, along_rows, along_cols)):
                 force = dcc * slope
                 for k in range(2):
@@ -283,41 +290,62 @@
         lane_row = iota((1, 128), 1)
         return jnp.where(lane_row == PLACE_LANE, place.astype(F32) * 0.25, row)
 
-    def exchange(source, targets, everything, sem, partners):
-        for d, peer in enumerate(partners):
+    unsent = []
+
+    def exchange(source, targets, sem, partners):
+        for index, peer in enumerate(partners):
             pltpu.make_async_remote_copy(
-                source, targets.at[d + 1], gather_send.at[sem], gather_recv.at[sem],
+                source, targets.at[index], gather_send.at[sem], gather_recv.at[sem],
                 device_id=peer, device_id_type=MESH,
             ).start()
-        return pltpu.make_async_remote_copy(
-            everything, everything, gather_send.at[sem], gather_recv.at[sem],
+        done = pltpu.make_async_remote_copy(
+            targets, targets, gather_send.at[sem], gather_recv.at[sem],
             device_id=partners[0], device_id_type=MESH,
         )
+        unsent.append(done)
+        return done
 
     def start_gather(turn, row):
-        mine, every = rows_y.at[turn], rows.at[turn]
         rows_y[turn, 0] = row
-        done_y = exchange(mine.at[0], mine, mine.at[1:NY], 2 * turn, along_y)
+        summed = exchange(rows_y.at[turn, 0], rows_y.at[turn, 1:NY], 2 * turn, along_y)
         if turn == 0:
-            pl.semaphore_wait(known.at[1], 2)
-        done_y.wait_recv()
-        rows[turn, 0] = (rows_y[turn, 0] + rows_y[turn, 2]) + (rows_y[turn, 1] + rows_y[turn, 3])
-        return done_y, exchange(every.at[0], every, every.at[1:128], 2 * turn + 1, others)
-
-    for chunk in range(2):
-        at = pl.ds(16 * chunk, 16)
-        fixed = [image_i[p, at, :] for p in (0, 1, 2, 3, 12, 13, 14, 15)]
-        moved = [image_j[1 + p, at, :] for p in (0, 1, 2, 3, 12, 13, 14, 15)]
-        for slot, planes in enumerate(products(fixed, moved)):
-            inner = [inner_sums[slot, p, at, :] for p in range(8)]
-            put_sums(slot, chunk, inner, side_sums(planes[:4], planes[4:]))
+            pl.semaphore_wait(known.at[2], 2)
+            tell(3)
+        summed.wait_recv()
+        every = rows.at[turn]
+        rows[turn, 0] = (rows_y[turn, 0] + rows_y[turn, 1]) + (rows_y[turn, 2] + rows_y[turn, 3])
+        if turn == 0:
+            pl.semaphore_wait(known.at[3], 2)
+        return exchange(every.at[0], every.at[1:128], 2 * turn + 1, others)
+
+    def finish_gather(turn, done):
+        done.wait_recv()
+        return rows[turn].reshape(128, 128)
+
+    def first_sums(slots):
+        for chunk in range(2):
+            at = pl.ds(16 * chunk, 16)
+            fixed = [image_i[p, at, :] for p in (0, 1, 2, 3, 12, 13, 14, 15)]
+            moved = [image_j[1 + p, at, :] for p in (0, 1, 2, 3, 12, 13, 14, 15)]
+            for slot, planes in enumerate(products(fixed, moved)):
+                if slot in slots:
+                    inner = [inner_sums[slot, p, at, :] for p in range(8)]
+                    put_sums(slot, chunk, inner, side_sums(planes[:4], planes[4:]))
+
+    first_sums((0, 1))
     mean_i = box_sums(0)
     stat_i[0] = mean_i
     stat_i[1] = box_sums(1) - mean_i * mean_i
+    for copy in halos[2:4]:
+        copy.wait_recv()
+    for p in range(4):
+        image_j[1 + p] = halo_j[0, 1 + p].astype(F32) * inside_low
+        image_j[13 + p] = halo_j[1, p].astype(F32) * inside_high
+    first_sums((2, 3, 4))
     for slot in range(3):
         means[slot] = box_sums(2 + slot)
     row = piece([image_j[1 + p] for p in range(16)], True)
-    first_y, first = start_gather(0, row)
+    waits = start_gather(0, row)
 
     own_row, own_col = place >> 3, place & 7
     r, c = iota((128, 128), 0), iota((128, 128), 1)
@@ -344,8 +372,7 @@
             flat, grad_cols[...], preferred_element_type=F32
         )
 
-    first.wait_recv()
-    gathered = rows[0].reshape(128, 128)
+    gathered = finish_gather(0, waits)
 
     spot = jnp.broadcast_to(gathered[:, PLACE_LANE : PLACE_LANE + 1], (128, 128))
     r, c = iota((128, 128), 0), iota((128, 128), 1)
@@ -371,20 +398,27 @@
         turned = pltpu.roll(gathered, 64, 1)
         right = lambda high, low: jnp.where(first_half, high, low - low.astype(BF16).astype(F32))
         both = jnp.concatenate([right(gathered, turned), right(turned, gathered)], axis=0)
-        value = jnp.dot(combine[start:352, :], both.astype(BF16), preferred_element_type=F32)
-        return value + pltpu.roll(value, 64, 1)
+        return jnp.dot(combine[start:352, :], both.astype(BF16), preferred_element_type=F32)
 
     def regular_of(grid):
-        cols = [grid[32 * col : 32 * col + 32] for col in range(8)]
+        low_lanes = first_half[0:16]
+        cols = []
+        for col in range(8):
+            top, bottom = grid[32 * col : 32 * col + 16], grid[32 * col + 16 : 32 * col + 32]
+            cols.append(
+                jnp.where(low_lanes, top, bottom)
+                + pltpu.roll(jnp.where(low_lanes, bottom, top), 64, 1)
+            )
         out = []
-        squares = jnp.zeros((32, 128), F32)
-        inside = (turns >= 1) & (turns <= 8) & (groups < 6) & (iota((32, 128), 1) < 64)
+        squares = jnp.zeros((16, 128), F32)
+        group, turn = groups[0:16], turns[0:16]
+        inside = (turn >= 1) & (turn <= 8) & (group < 6)
         for col in range(8):
             value = cols[col]
             if col > 0:
-                value = value + jnp.where(turns == 1, pltpu.roll(cols[col - 1], 120, 1), 0.0)
+                value = value + jnp.where(turn == 1, pltpu.roll(cols[col - 1], 120, 1), 0.0)
             if col < 7:
-                value = value + jnp.where(turns == 8, pltpu.roll(cols[col + 1], 8, 1), 0.0)
+                value = value + jnp.where(turn == 8, pltpu.roll(cols[col + 1], 8, 1), 0.0)
             value = jnp.where(inside, value, 0.0)
             squares = squares + value * value
             out.append(value)
@@ -392,10 +426,11 @@
         return out, STEP_LENGTH / jnp.sqrt(mean + EPSILON)
 
     grid = combined(gathered, 0)
+    around = grid[0:96] + pltpu.roll(grid[0:96], 64, 1)
     half = first_half[0:32]
-    near = jnp.where(half, grid[0:32], grid[32:64])
+    near = jnp.where(half, around[0:32], around[32:64])
     high, low = split(near)
-    above_high, above_low = split(grid[64:96])
+    above_high, above_low = split(around[64:96])
     above = jnp.where(half, above_high.astype(F32), above_low.astype(F32)).astype(BF16)
     wide = jnp.concatenate([high, low, above], axis=1)
     group_wide = jnp.concatenate([groups, groups, groups], axis=1)
@@ -438,24 +473,21 @@
     for slot in range(3):
         means[slot] = box_sums(2 + slot)
     row = piece([warped_ref[p] for p in range(16)], False)
-    store = pltpu.make_async_copy(cc_ref, cc_hbm.at[0], local_sem.at[0])
-    store.start()
-    second_y, second = start_gather(1, row)
-    second.wait_recv()
-    regular, scale = regular_of(combined(rows[1].reshape(128, 128), 96))
+    waits = start_gather(1, row)
+    regular, scale = regular_of(combined(finish_gather(1, waits), 96))
     total = [before[col] + regular[col] * scale for col in range(8)]
-    lane_col = iota((32, 128), 1) >> 3
+    lane_col = (iota((16, 128), 1) >> 3) & 7
     for ck in range(6):
-        value = jnp.zeros((32, 128), F32)
+        value = jnp.zeros((16, 128), F32)
         for col in range(8):
             moved = pltpu.roll(total[col], (8 * col - WIDE * ck - 1) % 128, 1)
             value = jnp.where(lane_col == col, moved, value)
-        velocity_ref[ck // 2, ck % 2] = value[:, 0:64]
+        velocity_ref[ck // 2, ck % 2, 0:16, :] = value[:, 0:64]
+        velocity_ref[ck // 2, ck % 2, 16:32, :] = value[:, 64:128]
     for copy in halos:
         copy.wait_send()
-    for copy in (first_y, first, second_y, second):
+    for copy in unsent:
         copy.wait_send()
-    store.wait()
 
 
 def per_device(fixed, moving, block_place, tissue):
@@ -469,12 +501,12 @@
         in_specs=[
             pl.BlockSpec(memory_space=pltpu.HBM),
             pl.BlockSpec(memory_space=pltpu.HBM),
-            pl.BlockSpec(memory_space=pltpu.SMEM),
-            pl.BlockSpec(memory_space=pltpu.SMEM),
+            pl.BlockSpec(memory_space=pltpu.HBM),
+            pl.BlockSpec(memory_space=pltpu.HBM),
         ],
         out_specs=(
             pl.BlockSpec(memory_space=pltpu.VMEM),
-            pl.BlockSpec(memory_space=pl.ANY),
+            pl.BlockSpec(memory_space=pltpu.VMEM),
         ),
         scratch_shapes=[
             vmem((8, 32, 128), BF16),
@@ -496,17 +528,18 @@
             vmem((5, 256, 256), BF16),
             vmem((3, 256, 128), F32),
             vmem((2, 256, 128), F32),
-            vmem((8, 32, 128), F32),
             vmem((352, 256), BF16),
-            vmem((8, 32, 128), F32),
+            vmem((8, 16, 128), F32),
             vmem((2, NY, 1, 128), F32),
             vmem((2, 128, 1, 128), F32),
-            pltpu.SemaphoreType.DMA((2,)),
+            pltpu.SMEM((1,), jnp.int32),
+            pltpu.SMEM((1,), jnp.int32),
+            pltpu.SemaphoreType.DMA((4,)),
             pltpu.SemaphoreType.DMA((6,)),
             pltpu.SemaphoreType.DMA((6,)),
             pltpu.SemaphoreType.DMA((4,)),
             pltpu.SemaphoreType.DMA((4,)),
-            pltpu.SemaphoreType.REGULAR((2,)),
+            pltpu.SemaphoreType.REGULAR((len(ROUNDS),)),
         ],
         compiler_params=pltpu.CompilerParams(
             collective_id=0, has_side_effects=True, vmem_limit_bytes=32 * 1024 * 1024

time: 48.3 us -> 47.3 us (0.979)
  Pallas kernels: 45 us -> 43.9 us
    pallas_call x1, Pallas kernels: 45 us -> 43.9 us  [per_device(): pl.pallas_call(kernel, out_shape=(jax.ShapeDtypeStruct((3, 2, 32, 64), F3...]
where the time goes in v4:
time: 47.3 us; the launch traced here: 47.1 us
  Pallas kernels  43.9 us (93%)
  between operations  1.93 us (4%)
  local copies, waits for them, and re-layouts  1.3 us (3%)
    pallas_call x1, Pallas kernels, per_device(): pl.pallas_call(kernel, out_shape=(jax.ShapeDtypeStruct((3, 2, 32, 64), F3...  43.9 us
    unnamed x2, local copies, waits for them, and re-layouts  1.3 us

profile of v4, /device:TPU:1, one launch (start us, length us, event | category | flops | bytes accessed | tf_op | source)
XLA Modules:
  0.0 47.1 jit_solution(17031864273723070180)
XLA Ops:
  1.9 43.9 %shard_map.59 = (f32[3,2,32,64]{3,2,1,0:T(8,128)S(1)}, f32[1,8,32,128]{3,2,1,0:T(8,128)S(1)}) custom-call(bf16[1,8,32,128]{3,2,1,0:T(8,128)(2,1)} %fixed_hbm.1, bf16[1,8,32,128]{3,2,1,0:T(8,128)(2,1)} %moving_hbm.1, s32[1]{0:T(128)S(6)} %copy.8.place_in, s32[1]{0:T(128)S(6)} %copy.9.tissue_in), custom_call_target="tpu_custom_call" | custom-call | tf_op jit(solution)/shard_map/pallas_call | solution.py:495
  45.8 0.6 %copy.10 = f32[3,2,32,64]{3,2,1,0:T(8,128)} copy(f32[3,2,32,64]{3,2,1,0:T(8,128)S(1)} %get-tuple-element.4) | data formatting | bytes 98304
  46.5 0.7 %copy.11 = f32[1,8,32,128]{3,2,1,0:T(8,128)} copy(f32[1,8,32,128]{3,2,1,0:T(8,128)S(1)} %get-tuple-element.5) | data formatting | bytes 262144

commit v5 on v4

--- a/solution.py
+++ b/solution.py
@@ -18,6 +18,7 @@
 WIDE = 10
 PLACE_LANE = 60
 MESH = pl.DeviceIdType.MESH
+OPPOSITE = 2 * NX
 ROUNDS = (1, 2, 4, 1)
 
 
@@ -41,7 +42,8 @@
     along_x = [(at_x[d // 2] + at_z[0] + at_core[d % 2], y) for d in range(1, 2 * NX)]
     along_z = {d: (at_x[0] + at_z[d % NZC] + core, y) for d in (1, 2, 4, -1, -2, -4)}
     others = [(at_x[dx] + at_z[dz] + at_core[dc], y) for dz, dx, dc in far_first()]
-    return along_y, along_x, along_z, others
+    opposite = [(peer, (y + d) % NY) for peer, _ in others[:OPPOSITE] for d in range(NY)]
+    return along_y, along_x, along_z, others, opposite
 
 
 def iota(shape, dim):
@@ -118,10 +120,10 @@
     image_i, image_j, slope_x, slope_y, warped_ref,
     box_rows, box_cols, grad_rows, grad_cols, gauss_cols, to_cols,
     inner_sums, sums, means, stat_i, combine, before,
-    rows_y, rows, place_ref, tissue_ref, local_sem, halo_send, halo_recv, gather_send, gather_recv, known,
+    rows_y, rows, unsummed, place_ref, tissue_ref, local_sem, halo_send, halo_recv, gather_send, gather_recv, known,
 ):
     gz = lax.axis_index("gz")
-    along_y, along_x, along_z, others = peers()
+    along_y, along_x, along_z, others, opposite = peers()
     next_z = [along_z[1], along_z[-1]]
     barrier = pltpu.get_barrier_semaphore()
     for peer in along_y + along_x + next_z:
@@ -308,6 +310,8 @@
     def start_gather(turn, row):
         rows_y[turn, 0] = row
         summed = exchange(rows_y.at[turn, 0], rows_y.at[turn, 1:NY], 2 * turn, along_y)
+        waits = [exchange(rows_y.at[turn, 0], unsummed, 4, opposite)] if turn == 1 else []
+        skip = OPPOSITE if turn == 1 else 0
         if turn == 0:
             pl.semaphore_wait(known.at[2], 2)
             tell(3)
@@ -316,10 +320,15 @@
         rows[turn, 0] = (rows_y[turn, 0] + rows_y[turn, 1]) + (rows_y[turn, 2] + rows_y[turn, 3])
         if turn == 0:
             pl.semaphore_wait(known.at[3], 2)
-        return exchange(every.at[0], every.at[1:128], 2 * turn + 1, others)
-
-    def finish_gather(turn, done):
-        done.wait_recv()
+        done = exchange(every.at[0], every.at[1 + skip : 128], 2 * turn + 1, others[skip:])
+        return [done] + waits
+
+    def finish_gather(turn, waits):
+        for done in waits:
+            done.wait_recv()
+        if turn == 1:
+            four = unsummed[...].reshape(OPPOSITE, NY, 1, 128)
+            rows[turn, 1 : 1 + OPPOSITE] = (four[:, 0] + four[:, 2]) + (four[:, 1] + four[:, 3])
         return rows[turn].reshape(128, 128)
 
     def first_sums(slots):
@@ -439,7 +448,6 @@
     regular, scale = regular_of(grid[96:352])
     for col in range(8):
         before[col] = regular[col] * scale
-    moves = moves * scale
     shift = []
     for c in range(3):
         value, other = moves[64 * c : 64 * c + 32], moves[64 * c + 32 : 64 * c + 64]
@@ -448,14 +456,13 @@
     for p in range(16):
         deep = (gz * 8 + (p - 4)).astype(F32)
         part = jnp.clip((deep + 0.5) * (1.0 / 16.0) - 0.5, 0.0, 1.0)
-        value = image_j[1 + p]
         slopes = (
             0.5 * (image_j[2 + p] - image_j[p]),
             slope_x[32 * p : 32 * p + 32, :],
             slope_y[32 * p : 32 * p + 32, :],
         )
-        for (base, rise), slope in zip(shift, slopes):
-            value = value + (base + part * rise) * slope
+        change = sum((base + part * rise) * slope for (base, rise), slope in zip(shift, slopes))
+        value = image_j[1 + p] + scale * change
         if p < 4:
             value = value * inside_low
         if p >= 12:
@@ -532,13 +539,14 @@
             vmem((8, 16, 128), F32),
             vmem((2, NY, 1, 128), F32),
             vmem((2, 128, 1, 128), F32),
+            vmem((OPPOSITE * NY, 1, 128), F32),
             pltpu.SMEM((1,), jnp.int32),
             pltpu.SMEM((1,), jnp.int32),
             pltpu.SemaphoreType.DMA((4,)),
             pltpu.SemaphoreType.DMA((6,)),
             pltpu.SemaphoreType.DMA((6,)),
-            pltpu.SemaphoreType.DMA((4,)),
-            pltpu.SemaphoreType.DMA((4,)),
+            pltpu.SemaphoreType.DMA((5,)),
+            pltpu.SemaphoreType.DMA((5,)),
             pltpu.SemaphoreType.REGULAR((len(ROUNDS),)),
         ],
         compiler_params=pltpu.CompilerParams(

time: 47.3 us -> 46.9 us (level)
  no operation moved by 1% of the time
where the time goes in v5:
time: 46.9 us; the launch traced here: 46.7 us
  Pallas kernels  43.5 us (93%)
  between operations  1.93 us (4%)
  local copies, waits for them, and re-layouts  1.3 us (3%)
    pallas_call x1, Pallas kernels, per_device(): pl.pallas_call(kernel, out_shape=(jax.ShapeDtypeStruct((3, 2, 32, 64), F3...  43.5 us
    unnamed x2, local copies, waits for them, and re-layouts  1.3 us

profile of v5, /device:TPU:1, one launch (start us, length us, event | category | flops | bytes accessed | tf_op | source)
XLA Modules:
  0.0 46.7 jit_solution(6582654579171485488)
XLA Ops:
  1.9 43.5 %shard_map.59 = (f32[3,2,32,64]{3,2,1,0:T(8,128)S(1)}, f32[1,8,32,128]{3,2,1,0:T(8,128)S(1)}) custom-call(bf16[1,8,32,128]{3,2,1,0:T(8,128)(2,1)} %fixed_hbm.1, bf16[1,8,32,128]{3,2,1,0:T(8,128)(2,1)} %moving_hbm.1, s32[1]{0:T(128)S(6)} %copy.8.place_in, s32[1]{0:T(128)S(6)} %copy.9.tissue_in), custom_call_target="tpu_custom_call" | custom-call | tf_op jit(solution)/shard_map/pallas_call | solution.py:502
  45.4 0.6 %copy.10 = f32[3,2,32,64]{3,2,1,0:T(8,128)} copy(f32[3,2,32,64]{3,2,1,0:T(8,128)S(1)} %get-tuple-element.4) | data formatting | bytes 98304
  46.1 0.7 %copy.11 = f32[1,8,32,128]{3,2,1,0:T(8,128)} copy(f32[1,8,32,128]{3,2,1,0:T(8,128)S(1)} %get-tuple-element.5) | data formatting | bytes 262144

commit v6 on v5

--- a/solution.py
+++ b/solution.py
@@ -185,6 +185,8 @@
 
     inside_low = jnp.where(gz > 0, 1.0, 0.0)
     inside_high = jnp.where(gz < NY - 1, 1.0, 0.0)
+    pl.semaphore_wait(known.at[0], 2)
+    tell(1)
     load_j.wait()
     load_i.wait()
     load_place.wait()
@@ -228,8 +230,6 @@
             for p, value in enumerate(own_sums(planes)):
                 inner_sums[slot, p, at, :] = value
 
-    pl.semaphore_wait(known.at[0], 2)
-    tell(1)
     pl.semaphore_wait(known.at[1], 2)
     tell(2)
 

time: 46.9 us -> 46.9 us (level)
  no operation moved by 1% of the time
where the time goes in v6:
time: 46.9 us; the launch traced here: 46.7 us
  Pallas kernels  43.5 us (93%)
  between operations  1.93 us (4%)
  local copies, waits for them, and re-layouts  1.3 us (3%)
    pallas_call x1, Pallas kernels, per_device(): pl.pallas_call(kernel, out_shape=(jax.ShapeDtypeStruct((3, 2, 32, 64), F3...  43.5 us
    unnamed x2, local copies, waits for them, and re-layouts  1.3 us

profile of v6, /device:TPU:1, one launch (start us, length us, event | category | flops | bytes accessed | tf_op | source)
XLA Modules:
  0.0 46.7 jit_solution(18039190884890545123)
XLA Ops:
  1.9 43.5 %shard_map.59 = (f32[3,2,32,64]{3,2,1,0:T(8,128)S(1)}, f32[1,8,32,128]{3,2,1,0:T(8,128)S(1)}) custom-call(bf16[1,8,32,128]{3,2,1,0:T(8,128)(2,1)} %fixed_hbm.1, bf16[1,8,32,128]{3,2,1,0:T(8,128)(2,1)} %moving_hbm.1, s32[1]{0:T(128)S(6)} %copy.8.place_in, s32[1]{0:T(128)S(6)} %copy.9.tissue_in), custom_call_target="tpu_custom_call" | custom-call | tf_op jit(solution)/shard_map/pallas_call | solution.py:502
  45.4 0.6 %copy.10 = f32[3,2,32,64]{3,2,1,0:T(8,128)} copy(f32[3,2,32,64]{3,2,1,0:T(8,128)S(1)} %get-tuple-element.4) | data formatting | bytes 98304
  46.1 0.7 %copy.11 = f32[1,8,32,128]{3,2,1,0:T(8,128)} copy(f32[1,8,32,128]{3,2,1,0:T(8,128)S(1)} %get-tuple-element.5) | data formatting | bytes 262144
